TPU v7x, 32 devices: a whole 2x2x4 slice. The times are simulated.
32 devices in a mesh: req: 8 (over z, core), tensor: 4 (over y, x).
Axes of the slice: x: 2, y: 2, z: 4, core: 2. Of those that a mesh axis runs over, the one named last changes fastest.
Arguments:
- text: bfloat16 [3072, 4096], P('req', 'tensor'), may hold values from -6 to 6
- patches: bfloat16 [64, 6, 6, 4096], P('req', None, None, 'tensor'), may hold values from -6 to 6
- grids: int32 [64, 2], replicated, may hold values from 2 to 6, as said below
- image_request: int32 [64], replicated, may hold values from 0 to 7, as said below
- slot_start: int32 [64], replicated, may hold values from 1 to 375, as said below
- vis_gain: bfloat16 [4096], P('tensor'), may hold values from 0.099609375 to 1.8984375
- dec_gain: bfloat16 [4096], replicated, may hold values from 0.099609375 to 1.8984375
- w_qkv: bfloat16 [4096, 3, 2048], P(None, None, 'tensor'), may hold values from -0.09375 to 0.09375
- w_out: bfloat16 [2048, 4096], P('tensor'), may hold values from -0.125 to 0.125
Outputs:
- layer_out: bfloat16 [3072, 4096], P('req', 'tensor')
Inputs may be any that keep to these rules, and one draw needn't show every extreme that they name: `grids`: heights and widths are even; some image has a 6 x 6 grid and some a 2 x 2 grid. `image_request`: the images of one index of req go to distinct requests, one to each. `slot_start`: the regions of 9 positions of the images of one request don't intersect and lie within the prompt; position 0 of every prompt lies outside them.
All inputs are finite; a program needn't handle non-finite values.
Results may differ from a plain program's by a relative error of at most 0.011.
Values may be sent and summed in bfloat16 or wider, within the bound.
No kernel may reach another device: no remote copies, remote signals or barrier semaphores. Data moves between devices by JAX's collectives and lax.ppermute only.
A program may use at most 64 MiB of HBM per device.

v0:
```python
import jax
import jax.numpy as jnp
from jax import lax
from jax.sharding import PartitionSpec as P

D = 4096
HD = 128


def pool_blocks(block):
    lead = block.shape[:-3]
    side = block.shape[-3]
    width = block.shape[-1]
    half = side // 2
    shaped = block.astype(jnp.float32).reshape(lead + (half, 2, half, 2, width))
    return shaped.mean(axis=(-4, -2)).reshape(lead + (half * half, width))


def body(text, patches, grids, image_request, slot_start, vis_gain, dec_gain, w_qkv, w_out):
    n_req = lax.axis_size("req")
    me_req = lax.axis_index("req")
    me_ten = lax.axis_index("tensor")
    img_dev, side, _, width = patches.shape
    half = side // 2
    region = half * half
    length = text.shape[0]
    gain_v = vis_gain.astype(jnp.float32)
    req_map = image_request.reshape(n_req, img_dev)
    pick = req_map == me_req
    has_img = jnp.any(pick, axis=1)
    start_src = jnp.sum(jnp.where(pick, slot_start.reshape(n_req, img_dev), 0), axis=1)
    grid_src = jnp.sum(jnp.where(pick[:, :, None], grids.reshape(n_req, img_dev, 2), 0), axis=1)
    own_map = lax.dynamic_slice_in_dim(image_request, me_req * img_dev, img_dev)
    onehot = (jnp.arange(n_req, dtype=jnp.int32)[:, None] == own_map[None, :]).astype(jnp.bfloat16)
    outgoing = jnp.einsum(
        "nk,kabw->nabw", onehot, patches, preferred_element_type=jnp.float32
    ).astype(jnp.bfloat16)
    received = lax.all_to_all(outgoing, "req", split_axis=0, concat_axis=0, tiled=True)
    pooled = pool_blocks(received)
    sums = lax.psum(jnp.sum(pooled * pooled, axis=-1), "tensor")
    arrived = (pooled * lax.rsqrt(sums / D + 1e-05)[..., None] * gain_v).astype(jnp.bfloat16)
    cells = jnp.arange(region, dtype=jnp.int32)
    row_i = cells // half
    col_j = cells % half
    height = grid_src[:, 0][:, None] // 2
    grid_w = grid_src[:, 1][:, None] // 2
    valid = has_img[:, None] & (row_i[None, :] < height) & (col_j[None, :] < grid_w)
    pos = jnp.where(valid, start_src[:, None] + row_i[None, :] * grid_w + col_j[None, :], length)
    rpos = jnp.where(has_img[:, None], start_src[:, None] + cells[None, :], length)
    img_rows = (
        jnp.zeros((length, width), jnp.bfloat16)
        .at[pos.reshape(-1)]
        .set(arrived.reshape(-1, width), mode="drop")
    )
    is_img = jnp.zeros((length,), bool).at[pos.reshape(-1)].set(True, mode="drop")
    in_region = jnp.zeros((length,), bool).at[rpos.reshape(-1)].set(True, mode="drop")
    key_ok = ~in_region | is_img
    x_in = jnp.where(is_img[:, None], img_rows, text)
    xf = x_in.astype(jnp.float32)
    heads_cols = w_qkv.shape[2]
    w_flat = w_qkv.reshape(w_qkv.shape[0], 3 * heads_cols)
    gain_d = dec_gain.astype(jnp.float32)
    sums_rows = lax.psum(jnp.sum(xf * xf, axis=-1), "tensor")
    gain_part = lax.dynamic_slice_in_dim(gain_d, me_ten * width, width)
    normed = (xf * lax.rsqrt(sums_rows / D + 1e-05)[:, None] * gain_part).astype(jnp.bfloat16)
    qkv = jnp.dot(
        lax.all_gather(normed, "tensor", axis=1, tiled=True),
        w_flat,
        preferred_element_type=jnp.float32,
    )
    heads_here = heads_cols // HD
    qkv = qkv.astype(jnp.bfloat16).reshape(length, 3, heads_here, HD)
    scores = jnp.einsum("qhd,khd->hqk", qkv[:, 0], qkv[:, 1], preferred_element_type=jnp.float32)
    scores = scores / jnp.sqrt(jnp.float32(HD))
    causal = jnp.arange(length)[:, None] >= jnp.arange(length)[None, :]
    mask = causal & key_ok[None, :]
    scores = jnp.where(mask[None], scores, jnp.float32(-1e30))
    top = jnp.max(scores, axis=-1, keepdims=True)
    expo = jnp.exp(scores - top)
    probs = (expo / jnp.sum(expo, axis=-1, keepdims=True)).astype(jnp.bfloat16)
    context = jnp.einsum("hqk,khd->qhd", probs, qkv[:, 2], preferred_element_type=jnp.float32)
    context = context.astype(jnp.bfloat16).reshape(length, heads_cols)
    partial_value = jnp.dot(context, w_out, preferred_element_type=jnp.float32)
    summed = lax.psum_scatter(
        partial_value.astype(jnp.bfloat16), "tensor", scatter_dimension=1, tiled=True
    ).astype(jnp.float32)
    return (xf + summed).astype(jnp.bfloat16)


def solution(mesh):
    in_specs = (
        P("req", "tensor"),
        P("req", None, None, "tensor"),
        P(),
        P(),
        P(),
        P("tensor"),
        P(),
        P(None, None, "tensor"),
        P("tensor", None),
    )
    out_specs = P("req", "tensor")
    return jax.shard_map(body, mesh=mesh, in_specs=in_specs, out_specs=out_specs, check_vma=False)
```

profile of v0, /device:TPU:0, one launch (start us, length us, event | category | flops | bytes accessed | tf_op | source)
XLA Modules:
  0.0 182.0 jit_solution(1979492984602648749)
XLA Ops:
  6.5 0.0 copy-start
  6.5 0.0 copy-start.6
  6.5 0.0 copy-start.4
  6.5 0.0 copy-start.5
  6.6 0.8 dynamic_slice.6
  7.3 0.3 copy-done
  7.6 0.3 convolution_convert_fusion.2
  7.9 1.2 copy.43
  9.1 6.3 %all-to-all-start = ((bf16[8,6,6,1024]{3,2,1,0:T(8,128)(2,1)}), bf16[8,6,6,1024]{3,2,1,0:T(8,128)(2,1)S(1)}, u32[]{:S(2)}, u32[]{:S(2)}) async-start(bf16[8,6,6,1024]{3,2,1,0:T(8,128)(2,1)} %copy.43), calls=%async_computation | async-start | bytes 1572864 | tf_op jit(solution)/shard_map/all_to_all | solution.py:38
  15.5 0.0 all-gather.2.cloned.1.call-start
  15.5 0.0 copy-done.6
  15.5 0.1 eq.30
  15.6 0.0 copy-done.4
  15.6 0.1 reshape.242
  15.7 0.2 select_reduce_fusion
  15.9 0.1 lt.100
  15.9 0.1 lt.101
  16.0 0.1 lt.107
  16.1 0.1 lt.108
  16.2 0.0 copy-done.5
  16.2 0.1 reshape.243
  16.3 0.1 select_reduce_fusion.1
  16.4 0.1 add.121
  16.5 0.1 add.122
  16.5 0.1 reduce_or.9
  16.7 0.1 and.72
  16.7 0.1 and.73
  16.9 0.1 lt.105
  17.0 0.1 lt.98
  17.0 0.1 add.133
  17.1 0.0 copy-done.3
  17.2 0.8 scatter_custom_fusion
  18.0 0.7 dynamic-slice_convert_fusion
  18.7 17.8 %all-to-all-done = bf16[8,6,6,1024]{3,2,1,0:T(8,128)(2,1)S(1)} async-done(((bf16[8,6,6,1024]{3,2,1,0:T(8,128)(2,1)}), bf16[8,6,6,1024]{3,2,1,0:T(8,128)(2,1)S(1)}, u32[]{:S(2)}, u32[]{:S(2)}) %all-to-all-start) | async-done | bytes 589856 | tf_op jit(solution)/shard_map/all_to_all | solution.py:38
  36.4 0.3 copy.44
  36.8 0.1 convert_reduce_fusion
  36.9 0.2 copy.45
  37.1 0.1 multiply_reduce_fusion
  37.2 0.1 reduce_sum.61
  37.4 0.1 copy.61
  37.4 9.9 %psum.14 = f32[8,9]{1,0:T(8,128)S(1)} all-reduce(f32[8,9]{1,0:T(8,128)S(1)} %copy.61), channel_id=1, replica_groups=mesh['req'=8,'tensor'=4] {'tensor'}, use_global_device_ids=true, to_apply=%region_6.7 | all-reduce | flops 72 | bytes 576 | tf_op jit(solution)/shard_map/psum | solution.py:40
  47.3 0.1 mul.75
  47.4 1.3 scatter_custom_fusion.1
  48.7 0.0 copy-done.2
  48.7 0.5 fusion.2
  49.2 7.9 %psum.15 = f32[384]{0:T(512)S(1)} all-reduce(f32[384]{0:T(512)S(1)} %get-tuple-element.5), channel_id=1, replica_groups=mesh['req'=8,'tensor'=4] {'tensor'}, use_global_device_ids=true, to_apply=%region_9.10 | all-reduce | flops 384 | bytes 3072 | tf_op jit(solution)/shard_map/psum | solution.py:63
  57.1 1.1 fusion.4
  58.3 0.0 all-gather.2.cloned.1.call-update
  58.3 0.0 reduce-scatter.2.cloned.1.call-start
  58.3 17.0 %copy.49 = bf16[4096,3,512]{0,2,1:T(8,128)(2,1)} copy(bf16[4096,3,512]{2,0,1:T(8,128)(2,1)} %param.16) | data formatting | bytes 25165824 | tf_op args[7]
  75.3 1.0 scatter_custom_fusion.2
  76.4 0.1 fusion.9
  76.5 23.9 %all-gather.2.cloned.1.call-done = bf16[384,4096]{1,0:T(8,128)(2,1)} async-done(((bf16[384,1024]{1,0:T(8,128)(2,1)}), bf16[384,4096]{1,0:T(8,128)(2,1)}) %all-gather.2.cloned.1.call-update) | async-done | bytes 3145744 | tf_op jit(solution)/shard_map/all_gather | solution.py:67
  100.4 14.5 %convolution_convert_fusion.1 = bf16[384,1536]{1,0:T(8,128)(2,1)} fusion(bf16[384,4096]{1,0:T(8,128)(2,1)} %all-gather.2.cloned.1.call-done, bf16[4096,1536]{0,1:T(8,128)(2,1)} %bitcast.53), kind=kOutput, calls=%fused_computation.5 | convolution fusion | flops 4832428032 | bytes 16908288 | tf_op jit(solution)/shard_map/dot_general | solution.py:66
  114.9 2.5 %reshape.247 = bf16[384,3,4,128]{3,2,1,0:T(4,128)(2,1)S(1)} reshape(bf16[384,1536]{1,0:T(8,128)(2,1)} %convolution_convert_fusion.1) | data formatting | bytes 2359296 | tf_op jit(solution)/shard_map/reshape | solution.py:72
  117.4 1.2 fusion.29
  118.5 0.3 copy.58
  118.8 3.4 %fusion.30 = (f32[4,384]{1,0:T(4,128)S(1)}, f32[4,384,384]{1,2,0:T(8,128)}) fusion(pred[384,384]{0,1:T(8,128)(4,1)S(1)} %fusion.9, bf16[384,1,4,128]{3,2,1,0:T(4,128)(2,1)S(1)} %get-tuple-element.8, bf16[384,1,4,128]{3,2,1,0:T(4,128)(2,1)} %get-tuple-element.9), kind=kOutput, calls=%fused_computation.73 | convolution fusion | flops 153354624 | bytes 3299328 | tf_op jit(solution)/shard_map/sub | solution.py:79
  122.2 2.2 %convolution_convert_fusion.3 = bf16[4,128,384]{2,1,0:T(8,128)(2,1)S(1)} fusion(f32[4,384,384]{1,2,0:T(8,128)} %get-tuple-element.15, f32[4,384]{1,0:T(4,128)S(1)} %get-tuple-element.14, bf16[384,1,4,128]{0,3,2,1:T(8,128)(2,1)S(1)} %copy.58), kind=kOutput, calls=%fused_computation.18 | convolution fusion | flops 152371200 | bytes 3151872 | tf_op jit(solution)/shard_map/hqk,khd->qhd/dot_general | solution.py:81
  124.5 0.6 copy-done.1
  125.1 3.6 %convolution_convert_fusion = bf16[384,4096]{1,0:T(8,128)(2,1)} fusion(bf16[384,512]{0,1:T(8,128)(2,1)S(1)} %bitcast.55, bf16[512,4096]{1,0:T(8,128)(2,1)S(1)} %copy-done.1), kind=kOutput, calls=%fused_computation.4 | convolution fusion | flops 1612185600 | bytes 7733248 | tf_op jit(solution)/shard_map/dot_general | solution.py:83
  128.7 0.0 reduce-scatter.2.cloned.1.call-update
  128.7 44.1 %reduce-scatter.2.cloned.1.call-done = bf16[384,1024]{1,0:T(8,128)(2,1)} async-done(((bf16[384,4096]{1,0:T(8,128)(2,1)}), bf16[384,1024]{1,0:T(8,128)(2,1)}) %reduce-scatter.2.cloned.1.call-update) | async-done | bytes 786448 | tf_op jit(solution)/shard_map/reduce_scatter | solution.py:84
  172.8 2.3 %fusion.5 = bf16[384,1024]{1,0:T(8,128)(2,1)} fusion(bf16[384,1024]{1,0:T(8,128)(2,1)S(1)} %get-tuple-element.6, bf16[384,1024]{1,0:T(8,128)(2,1)} %reduce-scatter.2.cloned.1.call-done), kind=kLoop, calls=%fused_computation.16 | loop fusion | flops 1572864 | bytes 2359296 | tf_op jit(solution)/shard_map/convert_element_type | solution.py:87
  (17 shorter events, 0.1 us)
Async XLA Ops:
  6.5 1.1 copy-start
  6.5 9.0 %copy-start.6 = (s32[64]{0:T(128)S(1)}, s32[64]{0:T(128)}, u32[]{:S(2)}) copy-start(s32[64]{0:T(128)} %param.12) | copy-start | bytes 772
  6.5 9.1 %copy-start.4 = (s32[64,2]{0,1:T(2,128)S(1)}, s32[64,2]{0,1:T(2,128)}, u32[]{:S(2)}) copy-start(s32[64,2]{0,1:T(2,128)} %param.11) | copy-start | bytes 1540
  6.5 9.6 %copy-start.5 = (s32[64]{0:T(128)S(1)}, s32[64]{0:T(128)}, u32[]{:S(2)}) copy-start(s32[64]{0:T(128)} %param.13) | copy-start | bytes 772
  6.5 10.6 %copy-start.3 = (bf16[1024]{0:T(1024)(128)(2,1)S(1)}, bf16[1024]{0:T(1024)(128)(2,1)}, u32[]{:S(2)}) copy-start(bf16[1024]{0:T(1024)(128)(2,1)} %param.14) | copy-start | bytes 6148
  9.1 27.3 %all-to-all-start = ((bf16[8,6,6,1024]{3,2,1,0:T(8,128)(2,1)}), bf16[8,6,6,1024]{3,2,1,0:T(8,128)(2,1)S(1)}, u32[]{:S(2)}, u32[]{:S(2)}) async-start(bf16[8,6,6,1024]{3,2,1,0:T(8,128)(2,1)} %copy.43), calls=%async_computation | async-start | bytes 1572864 | tf_op jit(solution)/shard_map/all_to_all | solution.py:38
  15.5 84.9 %all-gather.2.cloned.1.call-start = ((), (), s32[]{:S(2)}) async-start(), calls=%async_computation.2 | async-start | bytes 3932160 | tf_op jit(solution)/shard_map/all_gather | solution.py:67
  18.7 30.0 %copy-start.2 = (bf16[384,1024]{1,0:T(8,128)(2,1)S(1)}, bf16[384,1024]{1,0:T(8,128)(2,1)}, u32[]{:S(2)}) copy-start(bf16[384,1024]{1,0:T(8,128)(2,1)} %param.9) | copy-start | bytes 2359300
  58.3 114.5 %reduce-scatter.2.cloned.1.call-start = ((), (), s32[]{:S(2)}) async-start(), calls=%async_computation.3 | async-start | bytes 3932160 | tf_op jit(solution)/shard_map/reduce_scatter | solution.py:84
  122.2 2.9 %copy-start.1 = (bf16[512,4096]{1,0:T(8,128)(2,1)S(1)}, bf16[512,4096]{1,0:T(8,128)(2,1)}, u32[]{:S(2)}) copy-start(bf16[512,4096]{1,0:T(8,128)(2,1)} %param.17) | copy-start | bytes 12582916
Sparse Core Ops, SparseCore 0:
  58.4 41.9 all-gather.1
  128.8 43.9 reduce-scatter.1
where the time goes:
time: 183 us; the launch traced here: 182 us
  waiting for transfers between devices  85.8 us (47%)
  local copies, waits for them, and re-layouts  27.7 us (15%)
  matrix products  23.9 us (13%)
  blocking collectives  17.8 us (10%)
  between operations  13.6 us (7%)
  other arithmetic  6.68 us (4%)
  starting transfers between devices  6.4 us (3%)
    reduce_scatter x1, waiting for transfers between devices, body(): lax.psum_scatter(partial_value.astype(jnp.bfloat16), 'tensor', scatter_di...  44.1 us
    all_gather x1, waiting for transfers between devices, body(): lax.all_gather(normed, 'tensor', axis=1, tiled=True)  23.9 us
    unnamed x16, local copies, waits for them, and re-layouts  18.2 us
    all_to_all x1, waiting for transfers between devices, body(): lax.all_to_all(outgoing, 'req', split_axis=0, concat_axis=0, tiled=True)  17.8 us
    dot_general x1, matrix products, body(): jnp.dot(lax.all_gather(normed, 'tensor', axis=1, tiled=True), w_flat, pre...  14.5 us
    psum x1, blocking collectives, body(): sums = lax.psum(jnp.sum(pooled * pooled, axis=-1), 'tensor')  9.89 us
    psum x1, blocking collectives, body(): sums_rows = lax.psum(jnp.sum(xf * xf, axis=-1), 'tensor')  7.95 us
    all_to_all x1, starting transfers between devices, body(): lax.all_to_all(outgoing, 'req', split_axis=0, concat_axis=0, tiled=True)  6.33 us
  transfers between devices with their start and end apart: 3, of which 3 were waited for; matrix products, arithmetic and copies ran while one was open for 12% of the time, Pallas kernels for 0%

commit v1 on v0

v1 whole, which is shorter than its diff:
```python
import functools

import jax
import jax.numpy as jnp
from jax import lax
from jax.experimental import pallas as pl
from jax.experimental.pallas import tpu as pltpu
from jax.sharding import PartitionSpec as P

D = 4096
HD = 128
EPS = 1e-05


def round_up(n, m):
    return -(-n // m) * m


def swap(x, s):
    n = lax.axis_size("tensor")
    return lax.ppermute(x, "tensor", [(i, i ^ s) for i in range(n)])


def low_bit(s):
    return s & -s


def high_bit(s):
    return 1 << (s.bit_length() - 1)


def by_bits(n, reverse=False):
    return sorted(range(1, n), key=lambda s: (bin(s).count("1"), s), reverse=reverse)


def gather_halves(top, bottom, n):
    blocks = {0: (top, bottom)}
    for s in by_bits(n):
        low, high = low_bit(s), high_bit(s)
        if low == high:
            other = (swap(top, s), swap(bottom, s))
        else:
            other = (swap(blocks[s ^ low][0], low), swap(blocks[s ^ high][1], high))
        blocks[s] = other
    return blocks


def vmem_specs(n):
    return [pl.BlockSpec(memory_space=pltpu.VMEM)] * n


def params(mib):
    return pltpu.CompilerParams(vmem_limit_bytes=mib * 1024 * 1024)


def pool_kernel(map_ref, x_ref, out_ref, tmp_ref):
    n_req, region = out_ref.shape[0], tmp_ref.shape[1]
    side, img_dev = x_ref.shape[0], x_ref.shape[2]
    half = side // 2
    rows = lax.broadcasted_iota(jnp.int32, (n_req, img_dev), 0)
    onehot = (rows == map_ref[0:1, :]).astype(jnp.bfloat16)
    tmp_ref[...] = jnp.zeros_like(tmp_ref)
    for i in range(half):
        for j in range(half):
            total = x_ref[2 * i, 2 * j].astype(jnp.float32)
            for a, b in ((0, 1), (1, 0), (1, 1)):
                total += x_ref[2 * i + a, 2 * j + b].astype(jnp.float32)
            pooled = (total * 0.25).astype(jnp.bfloat16)
            tmp_ref[:, i * half + j, :] = jnp.dot(onehot, pooled, preferred_element_type=jnp.float32)
    out_ref[...] = tmp_ref[...].astype(jnp.bfloat16)


def pool_images(own_map, patches, n_req):
    side, _, img_dev, width = patches.shape
    padded = round_up((side // 2) ** 2, 16)
    return pl.pallas_call(
        pool_kernel,
        out_shape=jax.ShapeDtypeStruct((n_req, padded, width), jnp.bfloat16),
        in_specs=vmem_specs(2),
        out_specs=pl.BlockSpec(memory_space=pltpu.VMEM),
        scratch_shapes=[pltpu.VMEM((n_req, padded, width), jnp.float32)],
        compiler_params=params(24),
        cost_estimate=pl.CostEstimate(flops=0, bytes_accessed=4 * side * side * img_dev * width, transcendentals=0),
    )(jnp.broadcast_to(own_map[None, :], (8, img_dev)), patches)


def pack_kernel(region, rec_ref, gain_ref, out_ref, tmp_ref):
    n_req = rec_ref.shape[0]
    for r in range(n_req):
        tmp_ref[region * r : region * (r + 1)] = rec_ref[r].astype(jnp.float32)[:region]
    rest = tmp_ref.shape[0] - region * n_req
    tmp_ref[region * n_req :] = jnp.broadcast_to(gain_ref[0:1, :], (rest, gain_ref.shape[1]))
    out_ref[...] = tmp_ref[...].astype(jnp.bfloat16)


def pack_images(received, gain, region, n_img):
    width = received.shape[2]
    return pl.pallas_call(
        functools.partial(pack_kernel, region),
        out_shape=jax.ShapeDtypeStruct((n_img, width), jnp.bfloat16),
        in_specs=vmem_specs(2),
        out_specs=pl.BlockSpec(memory_space=pltpu.VMEM),
        scratch_shapes=[pltpu.VMEM((n_img, width), jnp.float32)],
        compiler_params=params(24),
        cost_estimate=pl.CostEstimate(flops=0, bytes_accessed=4 * n_img * width, transcendentals=0),
    )(received, gain)


def weight_copies(n_blk, idx_ref, w_ref, wbuf_ref, sem_ref):
    width = wbuf_ref.shape[2]
    copies = []
    for s in range(n_blk):
        first = pl.multiple_of(idx_ref[s] * width, width)
        copies.append(
            [
                pltpu.make_async_copy(w_ref.at[j, pl.ds(first, width)], wbuf_ref.at[s, j], sem_ref.at[s, j])
                for j in range(3)
            ]
        )
    for row in copies:
        for copy in row:
            copy.start()
    return copies


def weight_scratch(n_blk, width, cols):
    return [pltpu.VMEM((n_blk, 3, width, cols), jnp.bfloat16), pltpu.SemaphoreType.DMA((n_blk, 3))]


def text_kernel(n_blk, has_acc, idx_ref, *refs):
    x_refs, refs = refs[: 2 * n_blk], refs[2 * n_blk :]
    if has_acc:
        gain_ref, w_ref, acc_in, ss_in, acc_ref, ss_ref, wbuf_ref, sem_ref = refs
    else:
        gain_ref, w_ref, acc_ref, ss_ref, wbuf_ref, sem_ref = refs
    half = x_refs[0].shape[0]
    copies = weight_copies(n_blk, idx_ref, w_ref, wbuf_ref, sem_ref)
    scaled = []
    for side in range(2):
        rows = pl.ds(side * half, half)
        total = ss_in[rows] if has_acc else jnp.zeros((half, 128), jnp.float32)
        for s in range(n_blk):
            xf = x_refs[2 * s + side][...].astype(jnp.float32)
            scaled.append((xf * gain_ref[s]).astype(jnp.bfloat16))
            total += jnp.sum(xf * xf, axis=1, keepdims=True)
        ss_ref[rows] = total
    for s in range(n_blk):
        for j in range(3):
            copies[s][j].wait()
            for side in range(2):
                rows = pl.ds(side * half, half)
                prod = jnp.dot(scaled[side * n_blk + s], wbuf_ref[s, j], preferred_element_type=jnp.float32)
                if s > 0:
                    prod += acc_ref[j, rows]
                elif has_acc:
                    prod += acc_in[j, rows]
                acc_ref[j, rows] = prod


def text_part(idx, blocks, gain, w, acc=None, ss=None):
    n_blk = len(blocks)
    half, width = blocks[0][0].shape
    rows, cols = 2 * half, w.shape[2]
    has_acc = acc is not None
    args = [h for b in blocks for h in b] + [gain, w]
    in_specs = vmem_specs(2 * n_blk + 1) + [pl.BlockSpec(memory_space=pl.ANY)]
    if has_acc:
        args += [acc, ss]
        in_specs += vmem_specs(2)
    return pl.pallas_call(
        functools.partial(text_kernel, n_blk, has_acc),
        out_shape=(
            jax.ShapeDtypeStruct((3, rows, cols), jnp.float32),
            jax.ShapeDtypeStruct((rows, 128), jnp.float32),
        ),
        in_specs=[pl.BlockSpec(memory_space=pltpu.SMEM)] + in_specs,
        out_specs=tuple(vmem_specs(2)),
        scratch_shapes=weight_scratch(n_blk, width, cols),
        compiler_params=params(28),
        cost_estimate=pl.CostEstimate(
            flops=2 * n_blk * rows * width * 3 * cols,
            bytes_accessed=2 * n_blk * width * 3 * cols,
            transcendentals=0,
        ),
    )(idx, *args)


def image_kernel(n_blk, n_rows, idx_ref, *refs):
    x_refs, (gain_ref, w_ref, qkv_ref, own_ref, wbuf_ref, sem_ref) = refs[:n_blk], refs[n_blk:]
    copies = weight_copies(n_blk, idx_ref, w_ref, wbuf_ref, sem_ref)
    total = 0.0
    for s in range(n_blk):
        xf = x_refs[s][...].astype(jnp.float32)
        total += jnp.sum(xf * xf, axis=1, keepdims=True)
    scale = lax.rsqrt(total / D + EPS)
    total = 0.0
    scaled = []
    for s in range(n_blk):
        xf = x_refs[s][...].astype(jnp.float32)
        merged = (xf * scale * xf[n_rows : n_rows + 1]).astype(jnp.bfloat16)
        if s == 0:
            own_ref[...] = merged
        mf = merged.astype(jnp.float32)
        total += jnp.sum(mf * mf, axis=1, keepdims=True)
        scaled.append((mf * gain_ref[s]).astype(jnp.bfloat16))
    scale = lax.rsqrt(total / D + EPS)
    for j in range(3):
        acc = 0.0
        for s in range(n_blk):
            copies[s][j].wait()
            acc += jnp.dot(scaled[s], wbuf_ref[s, j], preferred_element_type=jnp.float32)
        qkv_ref[j] = (acc * scale).astype(jnp.bfloat16)


def image_part(idx, blocks, gain, w, n_rows):
    n_blk = len(blocks)
    n_img, width = blocks[0].shape
    cols = w.shape[2]
    return pl.pallas_call(
        functools.partial(image_kernel, n_blk, n_rows),
        out_shape=(
            jax.ShapeDtypeStruct((3, n_img, cols), jnp.bfloat16),
            jax.ShapeDtypeStruct((n_img, width), jnp.bfloat16),
        ),
        in_specs=[pl.BlockSpec(memory_space=pltpu.SMEM)]
        + vmem_specs(n_blk + 1)
        + [pl.BlockSpec(memory_space=pl.ANY)],
        out_specs=tuple(vmem_specs(2)),
        scratch_shapes=weight_scratch(n_blk, width, cols),
        compiler_params=params(28),
        cost_estimate=pl.CostEstimate(
            flops=2 * n_blk * n_img * width * 3 * cols,
            bytes_accessed=2 * n_blk * width * 3 * cols,
            transcendentals=0,
        ),
    )(idx, *blocks, gain, w)


def final_kernel(idx_ref, top_ref, bottom_ref, gain_ref, w_ref, acc_ref, ss_ref, img_ref, place_ref, text_row_ref,
                 key_ref, w_out_ref, ctx_ref, far_top_ref, far_bottom_ref, wbuf_ref, sem_ref, qkv_ref, wo_ref, wo_sem):
    half = top_ref.shape[0]
    rows, cols = 2 * half, ctx_ref.shape[1]
    width = wo_ref.shape[1]
    copies = weight_copies(1, idx_ref, w_ref, wbuf_ref, sem_ref)
    first = pl.multiple_of(idx_ref[0] * width, width)
    wo_copy = pltpu.make_async_copy(w_out_ref.at[:, pl.ds(first, width)], wo_ref, wo_sem)
    wo_copy.start()
    scaled, scales = [], []
    for side, x_ref in enumerate((top_ref, bottom_ref)):
        part = pl.ds(side * half, half)
        xf = x_ref[...].astype(jnp.float32)
        scaled.append((xf * gain_ref[0]).astype(jnp.bfloat16))
        total = ss_ref[part] + jnp.sum(xf * xf, axis=1, keepdims=True)
        scales.append((lax.rsqrt(total / D + EPS) * text_row_ref[part])[:, :1])
    for j in range(3):
        copies[0][j].wait()
        for side in range(2):
            part = pl.ds(side * half, half)
            prod = jnp.dot(scaled[side], wbuf_ref[0, j], preferred_element_type=jnp.float32)
            put = jnp.dot(place_ref[part], img_ref[j], preferred_element_type=jnp.float32)
            qkv_ref[j, part] = ((prod + acc_ref[j, part]) * scales[side] + put).astype(jnp.bfloat16)
    step = 128
    for h in range(cols // HD):
        lanes = pl.ds(h * HD, HD)
        for r in range(rows // step):
            last = (r + 1) * step
            q = qkv_ref[0, pl.ds(r * step, step), lanes]
            k = qkv_ref[1, pl.ds(0, last), lanes]
            v = qkv_ref[2, pl.ds(0, last), lanes]
            scores = lax.dot_general(q, k, (((1,), (1,)), ((), ())), preferred_element_type=jnp.float32)
            scores = scores * (1.0 / HD**0.5)
            row = lax.broadcasted_iota(jnp.int32, (step, last), 0) + r * step
            col = lax.broadcasted_iota(jnp.int32, (step, last), 1)
            mask = (row >= col) & (key_ref[0:1, pl.ds(0, last)] > 0.5)
            scores = jnp.where(mask, scores, -1e30)
            top = jnp.max(scores, axis=1, keepdims=True)
            expo = jnp.exp(scores - top)
            probs = (expo / jnp.sum(expo, axis=1, keepdims=True)).astype(jnp.bfloat16)
            ctx_ref[pl.ds(r * step, step), lanes] = jnp.dot(
                probs, v, preferred_element_type=jnp.float32
            ).astype(jnp.bfloat16)
    wo_copy.wait()
    for side, out_ref in enumerate((far_top_ref, far_bottom_ref)):
        out_ref[...] = jnp.dot(
            ctx_ref[pl.ds(side * half, half)], wo_ref[...], preferred_element_type=jnp.float32
        ).astype(jnp.bfloat16)


def final_part(idx, block, gain, w, acc, ss, img, place, text_row, key_ok, w_out):
    half, width = block[0].shape
    rows, cols = 2 * half, w.shape[2]
    any_spec = pl.BlockSpec(memory_space=pl.ANY)
    return pl.pallas_call(
        final_kernel,
        out_shape=(
            jax.ShapeDtypeStruct((rows, cols), jnp.bfloat16),
            jax.ShapeDtypeStruct((half, width), jnp.bfloat16),
            jax.ShapeDtypeStruct((half, width), jnp.bfloat16),
        ),
        in_specs=[pl.BlockSpec(memory_space=pltpu.SMEM)]
        + vmem_specs(3)
        + [any_spec]
        + vmem_specs(6)
        + [any_spec],
        out_specs=tuple(vmem_specs(3)),
        scratch_shapes=weight_scratch(1, width, cols)
        + [
            pltpu.VMEM((3, rows, cols), jnp.bfloat16),
            pltpu.VMEM((cols, width), jnp.bfloat16),
            pltpu.SemaphoreType.DMA,
        ],
        compiler_params=params(28),
        cost_estimate=pl.CostEstimate(
            flops=2 * rows * width * 4 * cols + 4 * cols * rows * rows,
            bytes_accessed=2 * width * 4 * cols,
            transcendentals=cols // HD * rows * rows,
        ),
    )(idx, *block, gain, w, acc, ss, img, place, text_row, key_ok, w_out)


def out_kernel(idx_ref, ctx_ref, w_ref, top_ref, bottom_ref, wo_ref, wo_sem):
    half, width = top_ref.shape
    first = pl.multiple_of(idx_ref[0] * width, width)
    wo_copy = pltpu.make_async_copy(w_ref.at[:, pl.ds(first, width)], wo_ref, wo_sem)
    wo_copy.start()
    wo_copy.wait()
    for side, out_ref in enumerate((top_ref, bottom_ref)):
        out_ref[...] = jnp.dot(
            ctx_ref[pl.ds(side * half, half)], wo_ref[...], preferred_element_type=jnp.float32
        ).astype(out_ref.dtype)


def out_part(idx, ctx, w, width, dtype=jnp.bfloat16):
    rows, depth = ctx.shape
    return pl.pallas_call(
        out_kernel,
        out_shape=(
            jax.ShapeDtypeStruct((rows // 2, width), dtype),
            jax.ShapeDtypeStruct((rows // 2, width), dtype),
        ),
        in_specs=[pl.BlockSpec(memory_space=pltpu.SMEM)] + vmem_specs(1) + [pl.BlockSpec(memory_space=pl.ANY)],
        out_specs=tuple(vmem_specs(2)),
        scratch_shapes=[pltpu.VMEM((depth, width), jnp.bfloat16), pltpu.SemaphoreType.DMA],
        compiler_params=params(16),
        cost_estimate=pl.CostEstimate(
            flops=2 * rows * depth * width,
            bytes_accessed=2 * depth * width,
            transcendentals=0,
        ),
    )(idx, ctx, w)


def add_kernel(n_top, base_ref, *refs):
    out_ref = refs[-1]
    half = out_ref.shape[0] // 2
    for side, terms in enumerate((refs[:n_top], refs[n_top:-1])):
        part = pl.ds(side * half, half)
        total = terms[0][...].astype(jnp.float32)
        for term in terms[1:]:
            total += term[...].astype(jnp.float32)
        out_ref[part] = (base_ref[part].astype(jnp.float32) + total).astype(out_ref.dtype)


def add_all(base, top, bottom):
    return pl.pallas_call(
        functools.partial(add_kernel, len(top)),
        out_shape=jax.ShapeDtypeStruct(base.shape, jnp.bfloat16),
        in_specs=vmem_specs(1 + len(top) + len(bottom)),
        out_specs=pl.BlockSpec(memory_space=pltpu.VMEM),
        compiler_params=params(16),
        cost_estimate=pl.CostEstimate(
            flops=0, bytes_accessed=2 * base.size * (2 + len(top)), transcendentals=0
        ),
    )(base, *top, *bottom)


def scatter_terms(parts, n):
    acc = {s: [[parts[s][0]], [parts[s][1]]] for s in range(n)}
    for s in by_bits(n, reverse=True):
        for side, bit in ((0, low_bit(s)), (1, high_bit(s))):
            terms = [t.astype(jnp.float32) for t in acc[s][side]]
            out = functools.reduce(lambda a, b: a + b, terms).astype(jnp.bfloat16)
            acc[s ^ bit][side].append(swap(out, bit))
    return acc[0]


def body(text, patches, grids, image_request, slot_start, vis_gain, dec_gain, w_qkv, w_out):
    n_req = lax.axis_size("req")
    n_ten = lax.axis_size("tensor")
    me_req = lax.axis_index("req")
    me_ten = lax.axis_index("tensor")
    img_dev, side, _, width = patches.shape
    half = side // 2
    region = half * half
    length = text.shape[0]
    w3 = jnp.transpose(w_qkv, (1, 0, 2))
    owners = jnp.stack([(me_ten ^ s).astype(jnp.int32) for s in range(n_ten)])
    gains = dec_gain.astype(jnp.float32).reshape(n_ten, 1, width)[owners]

    blocks = gather_halves(text[: length // 2], text[length // 2 :], n_ten)

    own_map = lax.dynamic_slice_in_dim(image_request, me_req * img_dev, img_dev)
    outgoing = pool_images(own_map, jnp.transpose(patches, (1, 2, 0, 3)), n_req)
    received = lax.all_to_all(outgoing, "req", split_axis=0, concat_axis=0, tiled=True)
    n_rows = n_req * region
    n_img = round_up(n_rows + 1, 16)
    img_own = pack_images(received, vis_gain.astype(jnp.float32).reshape(1, width), region, n_img)
    img_blocks = [img_own] + [swap(img_own, s) for s in range(1, n_ten)]
    near = [blocks[s] for s in by_bits(n_ten)[:-1]]
    img_blocks, near = lax.optimization_barrier((img_blocks, near))
    img_qkv, merged = image_part(owners, img_blocks, gains, w3, n_rows)

    pick = image_request.reshape(n_req, img_dev) == me_req
    has_img = jnp.any(pick, axis=1)
    start_src = jnp.sum(jnp.where(pick, slot_start.reshape(n_req, img_dev), 0), axis=1)
    grid_src = jnp.sum(jnp.where(pick[:, :, None], grids.reshape(n_req, img_dev, 2), 0), axis=1)
    cells = jnp.arange(region, dtype=jnp.int32)
    row_i = cells // half
    col_j = cells % half
    height = grid_src[:, 0][:, None] // 2
    grid_w = grid_src[:, 1][:, None] // 2
    valid = has_img[:, None] & (row_i[None, :] < height) & (col_j[None, :] < grid_w)
    pos = jnp.where(valid, start_src[:, None] + row_i[None, :] * grid_w + col_j[None, :], -1)
    rpos = jnp.where(has_img[:, None], start_src[:, None] + cells[None, :], -1)
    pos = jnp.pad(pos.reshape(-1), (0, n_img - n_rows), constant_values=-1)
    spots = jnp.arange(length, dtype=jnp.int32)
    hit = spots[:, None] == pos[None, :]
    place = hit.astype(jnp.bfloat16)
    is_img = jnp.any(hit, axis=1)
    in_region = jnp.any(rpos.reshape(-1)[:, None] == spots[None, :], axis=0)
    is_key = jnp.any(pos[:, None] == spots[None, :], axis=0)
    key_ok = jnp.broadcast_to((~in_region | is_key).astype(jnp.float32)[None, :], (8, length))
    text_row = jnp.broadcast_to(1.0 - is_img.astype(jnp.float32)[:, None], (length, 128))
    img_here = jnp.dot(place, merged, preferred_element_type=jnp.float32).astype(jnp.bfloat16)
    x_in = jnp.where(is_img[:, None], img_here, text)

    order = by_bits(n_ten)
    acc, ss = text_part(owners[:1], [blocks[0]], gains[:1], w3)
    near_at = jnp.array(order[:-1])
    acc, ss = text_part(owners[near_at], near, gains[near_at], w3, acc, ss)
    far = order[-1]
    context, far_top, far_bottom = final_part(
        owners[far][None], blocks[far], gains[far][None], w3, acc, ss, img_qkv, place, text_row, key_ok, w_out
    )
    parts = {far: (far_top, far_bottom)}
    for s in reversed([0] + order[:-1]):
        parts[s] = out_part(owners[s][None], context, w_out, width, jnp.float32 if s == 0 else jnp.bfloat16)
    top, bottom = scatter_terms(parts, n_ten)
    return add_all(x_in, top, bottom)


def solution(mesh):
    in_specs = (
        P("req", "tensor"),
        P("req", None, None, "tensor"),
        P(),
        P(),
        P(),
        P("tensor"),
        P(),
        P(None, None, "tensor"),
        P("tensor", None),
    )
    out_specs = P("req", "tensor")
    return jax.shard_map(body, mesh=mesh, in_specs=in_specs, out_specs=out_specs, check_vma=False)
```

time: 183 us -> 96.4 us (0.53)
  waiting for transfers between devices: 85.8 us -> 23.9 us
  Pallas kernels: 0 us -> 24.8 us
  matrix products: 23.9 us -> 0.35 us
  blocking collectives: 17.8 us -> 0 us
  starting transfers between devices: 6.4 us -> 23.3 us
  between operations: 13.6 us -> 0.4 us
  local copies, waits for them, and re-layouts: 27.7 us -> 21.9 us
  other arithmetic: 6.68 us -> 1.26 us
    reduce_scatter x1 -> x0, waiting for transfers between devices: 44.1 us -> none  [body(): lax.psum_scatter(partial_value.astype(jnp.bfloat16), 'tensor', scatter_di...]
    pallas_call x0 -> x10, Pallas kernels: none -> 24.8 us  [the longest x1 7.95 us: final_part(): pl.pallas_call(final_kernel, out_shape=(jax.ShapeDtypeStruct((rows, cols)...]
    all_gather x1 -> x0, waiting for transfers between devices: 23.9 us -> none  [body(): lax.all_gather(normed, 'tensor', axis=1, tiled=True)]
    dot_general x4 -> x1, matrix products: 20.6 us -> 0.35 us  [body(): jnp.dot(place, merged, preferred_element_type=jnp.float32)]
    ppermute x0 -> x15, starting transfers between devices: none -> 18 us  [swap(): return lax.ppermute(x, 'tensor', [(i, i ^ s) for i in range(n)])]
    psum x2 -> x0, blocking collectives: 17.8 us -> none  [the longest x1 9.89 us: body(): sums = lax.psum(jnp.sum(pooled * pooled, axis=-1), 'tensor')]
    ppermute x0 -> x15, waiting for transfers between devices: none -> 16.9 us  [swap(): return lax.ppermute(x, 'tensor', [(i, i ^ s) for i in range(n)])]
    all_to_all x1, waiting for transfers between devices: 17.8 us -> 6.98 us  [body(): lax.all_to_all(outgoing, 'req', split_axis=0, concat_axis=0, tiled=True)]
  transfers between devices with their start and end apart: 3 -> 16, of which waited for: 3 -> 4; matrix products, arithmetic and copies ran while one was open for 12% -> 5% of each run, Pallas kernels for 0% -> 16%
where the time goes in v1:
time: 96.4 us; the launch traced here: 95.9 us
  Pallas kernels  24.8 us (26%)
  waiting for transfers between devices  23.9 us (25%)
  starting transfers between devices  23.3 us (24%)
  local copies, waits for them, and re-layouts  21.9 us (23%)
  other arithmetic  1.26 us (1%)
    ppermute x15, starting transfers between devices, swap(): return lax.ppermute(x, 'tensor', [(i, i ^ s) for i in range(n)])  18 us
    ppermute x15, waiting for transfers between devices, swap(): return lax.ppermute(x, 'tensor', [(i, i ^ s) for i in range(n)])  16.9 us
    unnamed x52, local copies, waits for them, and re-layouts  16.9 us
    pallas_call x1, Pallas kernels, final_part(): pl.pallas_call(final_kernel, out_shape=(jax.ShapeDtypeStruct((rows, cols)...  7.95 us
    pallas_call x2, Pallas kernels, text_part(): pl.pallas_call(functools.partial(text_kernel, n_blk, has_acc), out_shape=...  7.26 us
    all_to_all x1, waiting for transfers between devices, body(): lax.all_to_all(outgoing, 'req', split_axis=0, concat_axis=0, tiled=True)  6.98 us
    all_to_all x1, starting transfers between devices, body(): lax.all_to_all(outgoing, 'req', split_axis=0, concat_axis=0, tiled=True)  5.31 us
    pallas_call x1, Pallas kernels, image_part(): pl.pallas_call(functools.partial(image_kernel, n_blk, n_rows), out_shape=...  4.88 us
  transfers between devices with their start and end apart: 16, of which 4 were waited for; matrix products, arithmetic and copies ran while one was open for 5% of the time, Pallas kernels for 16%

profile of v1, /device:TPU:0, one launch (start us, length us, event | category | flops | bytes accessed | tf_op | source)
XLA Modules:
  0.0 95.9 jit_solution(16274840406442555681)
XLA Ops:
  0.0 1.2 %fusion.9 = (bf16[192,1024]{1,0:T(8,128)(2,1)S(1)}, bf16[192,1024]{1,0:T(8,128)(2,1)S(1)}) fusion(bf16[384,1024]{1,0:T(8,128)(2,1)} %param.10), kind=kLoop, calls=%fused_computation.44 | loop fusion | bytes 1572864 | tf_op jit(solution)/shard_map/slice | solution.py:400
  1.3 3.0 %collective-permute-start.5 = (bf16[192,1024]{1,0:T(8,128)(2,1)S(1)}, bf16[192,1024]{1,0:T(8,128)(2,1)S(1)}, u32[]{:S(2)}, u32[]{:S(2)}) collective-permute-start(bf16[192,1024]{1,0:T(8,128)(2,1)S(1)} %get-tuple-element.52.refs_0_), channel_id=1, source_target_pairs={{0,2},{1,3},{2,0},{3,1},{4,6},{5,7},{6,4},{7,5},{8,10},{9,11},{10,... | collective-permute-start | bytes 1179656 | tf_op jit(solution)/shard_map/ppermute | solution.py:21
  4.3 1.5 %collective-permute-start.3 = (bf16[192,1024]{1,0:T(8,128)(2,1)S(1)}, bf16[192,1024]{1,0:T(8,128)(2,1)S(1)}, u32[]{:S(2)}, u32[]{:S(2)}) collective-permute-start(bf16[192,1024]{1,0:T(8,128)(2,1)S(1)} %get-tuple-element.52.refs_0_), channel_id=1, source_target_pairs={{0,1},{1,0},{2,3},{3,2},{4,5},{5,4},{6,7},{7,6},{8,9},{9,8},{10,11... | collective-permute-start | bytes 1179656 | tf_op jit(solution)/shard_map/ppermute | solution.py:21
  5.8 0.5 collective-permute-start.4
  6.4 0.7 dynamic_slice.3
  7.1 1.1 %copy-done.7 = bf16[8,6,6,1024]{3,0,2,1:T(8,128)(2,1)S(1)} copy-done((bf16[8,6,6,1024]{3,0,2,1:T(8,128)(2,1)S(1)}, bf16[8,6,6,1024]{3,0,2,1:T(8,128)(2,1)}, u32[]{:S(2)}) %copy-start.7) | copy-done | bytes 589848
  8.2 1.0 %shard_map.100 = bf16[8,16,1024]{2,1,0:T(8,128)(2,1)} custom-call(s32[8,8]{1,0:T(8,128)S(1)} %broadcast_in_dim.46.map_ref, bf16[6,6,8,1024]{3,2,1,0:T(8,128)(2,1)S(1)} %bitcast.30), custom_call_target="tpu_custom_call" | custom-call | bytes 1179648 | tf_op jit(solution)/shard_map/pallas_call | solution.py:76
  9.2 5.3 %all-to-all-start = ((bf16[8,16,1024]{2,1,0:T(8,128)(2,1)}), bf16[8,16,1024]{2,1,0:T(8,128)(2,1)S(1)}, u32[]{:S(2)}, u32[]{:S(2)}) async-start(bf16[8,16,1024]{2,1,0:T(8,128)(2,1)} %shard_map.100), calls=%async_computation | async-start | bytes 524288 | tf_op jit(solution)/shard_map/all_to_all | solution.py:404
  14.6 0.1 eq.57
  14.7 0.2 select_reduce_fusion
  15.0 0.1 lt.77
  15.1 0.1 lt.84
  15.3 0.1 select_reduce_fusion.1
  15.5 0.1 add.81
  15.6 0.1 reduce_or.36
  15.8 0.1 and.47
  15.9 0.1 lt.74
  15.9 0.1 lt.81
  16.0 0.1 add.88
  16.1 0.1 fusion.3
  16.2 0.2 fusion.1
  16.4 0.1 fusion.4
  16.5 0.1 fusion.6
  16.7 0.6 gather_fusion
  17.3 7.0 %all-to-all-done.rec_ref = bf16[8,16,1024]{2,1,0:T(8,128)(2,1)S(1)} async-done(((bf16[8,16,1024]{2,1,0:T(8,128)(2,1)}), bf16[8,16,1024]{2,1,0:T(8,128)(2,1)S(1)}, u32[]{:S(2)}, u32[]{:S(2)}) %all-to-all-start) | async-done | bytes 262176 | tf_op jit(solution)/shard_map/all_to_all | solution.py:404
  24.3 1.6 %collective-permute-start = (bf16[80,1024]{1,0:T(8,128)(2,1)S(1)}, bf16[80,1024]{1,0:T(8,128)(2,1)S(1)}, u32[]{:S(2)}, u32[]{:S(2)}) collective-permute-start(bf16[80,1024]{1,0:T(8,128)(2,1)S(1)} %shard_map.101.refs_0_), channel_id=1, source_target_pairs={{0,1},{1,0},{2,3},{3,2},{4,5},{5,4},{6,7},{7,6},{8,9},{9,8},{10,11... | collective-permute-start | bytes 491528 | tf_op jit(solution)/shard_map/ppermute | solution.py:21
  25.9 1.5 %collective-permute-start.1 = (bf16[80,1024]{1,0:T(8,128)(2,1)S(1)}, bf16[80,1024]{1,0:T(8,128)(2,1)S(1)}, u32[]{:S(2)}, u32[]{:S(2)}) collective-permute-start(bf16[80,1024]{1,0:T(8,128)(2,1)S(1)} %shard_map.101.refs_0_), channel_id=1, source_target_pairs={{0,2},{1,3},{2,0},{3,1},{4,6},{5,7},{6,4},{7,5},{8,10},{9,11},{10,... | collective-permute-start | bytes 491528 | tf_op jit(solution)/shard_map/ppermute | solution.py:21
  27.4 0.5 collective-permute-start.2
  28.0 0.6 gather_fusion.2
  28.5 0.6 gather_fusion.1
  29.2 1.6 %collective-permute-start.7 = (bf16[192,1024]{1,0:T(8,128)(2,1)S(1)}, bf16[192,1024]{1,0:T(8,128)(2,1)S(1)}, u32[]{:S(2)}, u32[]{:S(2)}) collective-permute-start(bf16[192,1024]{1,0:T(8,128)(2,1)S(1)} %collective-permute-done.5.refs_2_), channel_id=1, source_target_pairs={{0,1},{1,0},{2,3},{3,2},{4,5},{5,4},{6,7},{7,6},{8,9},{9,8},{10,11... | collective-permute-start | bytes 1179656 | tf_op jit(solution)/shard_map/ppermute | solution.py:21
  30.7 1.5 %collective-permute-start.8 = (bf16[192,1024]{1,0:T(8,128)(2,1)S(1)}, bf16[192,1024]{1,0:T(8,128)(2,1)}, u32[]{:S(2)}, u32[]{:S(2)}) collective-permute-start(bf16[192,1024]{1,0:T(8,128)(2,1)S(1)} %collective-permute-done.4.refs_1_), channel_id=1, source_target_pairs={{0,2},{1,3},{2,0},{3,1},{4,6},{5,7},{6,4},{7,5},{8,10},{9,11},{10,... | collective-permute-start | bytes 1179656 | tf_op jit(solution)/shard_map/ppermute | solution.py:21
  32.3 4.6 %copy-done = bf16[4096,3,512]{2,0,1:T(8,128)(2,1)S(1)} copy-done((bf16[4096,3,512]{2,0,1:T(8,128)(2,1)S(1)}, bf16[4096,3,512]{2,0,1:T(8,128)(2,1)}, u32[]{:S(2)}) %copy-start) | copy-done | bytes 12582936
  36.8 2.3 %shard_map.103 = (f32[3,384,512]{2,1,0:T(8,128)S(1)}, f32[384,128]{1,0:T(8,128)S(1)}) custom-call(s32[1]{0:T(128)} %bitcast.2.idx_ref, bf16[192,1024]{1,0:T(8,128)(2,1)S(1)} %get-tuple-element.52.refs_0_, bf16[192,1024]{1,0:T(8,128)(2,1)S(1)} %get-tuple-element.51.refs_1_, f32[1,1,1024]{2,1,0:T(1,128)S(1)} %get-tuple-element.53.refs_2_, ...), custom_call_target="tpu_custom_call" | custom-call | flops 1207959552 | bytes 3145728 | tf_op jit(solution)/shard_map/pallas_call | solution.py:170
  39.2 1.4 %copy-done.5 = f32[3,384,512]{2,1,0:T(8,128)} copy-done((f32[3,384,512]{2,1,0:T(8,128)}, f32[3,384,512]{2,1,0:T(8,128)S(1)}, u32[]{:S(2)}) %copy-start.5) | copy-done | bytes 2359320
  40.6 0.7 copy-done.14
  41.3 1.0 %copy-done.1 = bf16[4096,3,512]{2,0,1:T(8,128)(2,1)S(1)} copy-done((bf16[4096,3,512]{2,0,1:T(8,128)(2,1)S(1)}, bf16[4096,3,512]{2,0,1:T(8,128)(2,1)}, u32[]{:S(2)}) %copy-start.1) | copy-done | bytes 12582936
  42.3 0.9 copy-done.15
  43.2 4.9 %shard_map.102 = (bf16[3,80,512]{2,1,0:T(8,128)(2,1)S(1)}, bf16[80,1024]{1,0:T(8,128)(2,1)S(1)}) custom-call(s32[4]{0:T(128)S(1)} %pad_add_fusion.idx_ref, bf16[80,1024]{1,0:T(8,128)(2,1)S(1)} %shard_map.101.refs_0_, bf16[80,1024]{1,0:T(8,128)(2,1)S(1)} %collective-permute-done.refs_1_, bf16[80,1024]{1,0:T(8,128)(2,1)S(1)} %collective-permute-done.1.refs_2_, ...), custom_call_target="tpu_custom_call" | custom-call | flops 1006632960 | bytes 12582912 | tf_op jit(solution)/shard_map/pallas_call | solution.py:219
  48.1 0.7 copy-done.12
  48.8 1.7 %copy-done.6 = f32[3,384,512]{2,1,0:T(8,128)S(1)} copy-done((f32[3,384,512]{2,1,0:T(8,128)S(1)}, f32[3,384,512]{2,1,0:T(8,128)}, u32[]{:S(2)}) %copy-start.6) | copy-done | bytes 2359320
  50.5 5.0 %shard_map.104 = (f32[3,384,512]{2,1,0:T(8,128)S(1)}, f32[384,128]{1,0:T(8,128)S(1)}) custom-call(s32[2]{0:T(128)S(1)} %gather_fusion.1, bf16[192,1024]{1,0:T(8,128)(2,1)S(1)} %collective-permute-done.3.refs_0_, bf16[192,1024]{1,0:T(8,128)(2,1)S(1)} %collective-permute-done.4.refs_1_, bf16[192,1024]{1,0:T(8,128)(2,1)S(1)} %collective-permute-done.5.refs_2_, ...), custom_call_target="tpu_custom_call" | custom-call | flops 2415919104 | bytes 6291456 | tf_op jit(solution)/shard_map/pallas_call | solution.py:170
  55.5 1.4 %copy-done.3 = f32[3,384,512]{2,1,0:T(8,128)} copy-done((f32[3,384,512]{2,1,0:T(8,128)}, f32[3,384,512]{2,1,0:T(8,128)S(1)}, u32[]{:S(2)}) %copy-start.3) | copy-done | bytes 2359320
  56.9 0.7 copy-done.10
  57.6 0.1 broadcast_in_dim.48.text_row_ref
  57.8 1.7 %copy-done.4 = f32[3,384,512]{2,1,0:T(8,128)S(1)} copy-done((f32[3,384,512]{2,1,0:T(8,128)S(1)}, f32[3,384,512]{2,1,0:T(8,128)}, u32[]{:S(2)}) %copy-start.4) | copy-done | bytes 2359320
  59.4 1.0 %copy-done.11 = bf16[192,1024]{1,0:T(8,128)(2,1)S(1)} copy-done((bf16[192,1024]{1,0:T(8,128)(2,1)S(1)}, bf16[192,1024]{1,0:T(8,128)(2,1)}, u32[]{:S(2)}) %copy-start.11) | copy-done | bytes 393240
  60.4 8.0 %shard_map.105 = (bf16[384,512]{1,0:T(8,128)(2,1)S(1)}, bf16[192,1024]{1,0:T(8,128)(2,1)S(1)}, bf16[192,1024]{1,0:T(8,128)(2,1)S(1)}) custom-call(s32[1]{0:T(128)} %bitcast.5.idx_ref, bf16[192,1024]{1,0:T(8,128)(2,1)S(1)} %copy-done.11, bf16[192,1024]{1,0:T(8,128)(2,1)} %collective-permute-done.8.bottom_ref, f32[1,1,1024]{2,1,0:T(1,128)S(1)} %get-tuple-element.54.gain_ref, ...), custom_call_target="tpu_custom_call" | custom-call | flops 1912602624 | bytes 4194304 | tf_op jit(solution)/shard_map/pallas_call | solution.py:293
  68.4 0.6 collective-permute-start.13
  69.0 0.5 collective-permute-start.9
  69.5 0.9 shard_map.108
  70.5 1.6 %collective-permute-start.11 = (bf16[192,1024]{1,0:T(8,128)(2,1)S(1)}, bf16[192,1024]{1,0:T(8,128)(2,1)S(1)}, u32[]{:S(2)}, u32[]{:S(2)}) collective-permute-start(bf16[192,1024]{1,0:T(8,128)(2,1)S(1)} %get-tuple-element.46), channel_id=1, source_target_pairs={{0,1},{1,0},{2,3},{3,2},{4,5},{5,4},{6,7},{7,6},{8,9},{9,8},{10,11... | collective-permute-start | bytes 1179656 | tf_op jit(solution)/shard_map/ppermute | solution.py:21
  72.0 0.8 shard_map.107
  72.8 1.6 %collective-permute-start.12 = (bf16[192,1024]{1,0:T(8,128)(2,1)S(1)}, bf16[192,1024]{1,0:T(8,128)(2,1)S(1)}, u32[]{:S(2)}, u32[]{:S(2)}) collective-permute-start(bf16[192,1024]{1,0:T(8,128)(2,1)S(1)} %get-tuple-element.48), channel_id=1, source_target_pairs={{0,2},{1,3},{2,0},{3,1},{4,6},{5,7},{6,4},{7,5},{8,10},{9,11},{10,... | collective-permute-start | bytes 1179656 | tf_op jit(solution)/shard_map/ppermute | solution.py:21
  74.4 6.1 %collective-permute-done.13 = bf16[192,1024]{1,0:T(8,128)(2,1)S(1)} collective-permute-done((bf16[192,1024]{1,0:T(8,128)(2,1)S(1)}, bf16[192,1024]{1,0:T(8,128)(2,1)S(1)}, u32[]{:S(2)}, u32[]{:S(2)}) %collective-permute-start.13) | collective-permute-done | bytes 393248 | tf_op jit(solution)/shard_map/ppermute | solution.py:21
  80.5 0.1 add_convert_fusion
  80.7 0.6 collective-permute-start.14
  81.3 0.1 add_convert_fusion.1
  81.4 1.4 %collective-permute-start.10 = (bf16[192,1024]{1,0:T(8,128)(2,1)S(1)}, bf16[192,1024]{1,0:T(8,128)(2,1)S(1)}, u32[]{:S(2)}, u32[]{:S(2)}) collective-permute-start(bf16[192,1024]{1,0:T(8,128)(2,1)S(1)} %add_convert_fusion.1), channel_id=1, source_target_pairs={{0,2},{1,3},{2,0},{3,1},{4,6},{5,7},{6,4},{7,5},{8,10},{9,11},{10,... | collective-permute-start | bytes 1179656 | tf_op jit(solution)/shard_map/ppermute | solution.py:21
  82.8 0.4 fusion.base_ref
  83.1 0.7 shard_map.106
  83.9 5.6 %collective-permute-done.11.refs_2_ = bf16[192,1024]{1,0:T(8,128)(2,1)S(1)} collective-permute-done((bf16[192,1024]{1,0:T(8,128)(2,1)S(1)}, bf16[192,1024]{1,0:T(8,128)(2,1)S(1)}, u32[]{:S(2)}, u32[]{:S(2)}) %collective-permute-start.11) | collective-permute-done | bytes 393248 | tf_op jit(solution)/shard_map/ppermute | solution.py:21
  89.5 5.2 %collective-permute-done.14.refs_5_ = bf16[192,1024]{1,0:T(8,128)(2,1)S(1)} collective-permute-done((bf16[192,1024]{1,0:T(8,128)(2,1)S(1)}, bf16[192,1024]{1,0:T(8,128)(2,1)S(1)}, u32[]{:S(2)}, u32[]{:S(2)}) %collective-permute-start.14) | collective-permute-done | bytes 393248 | tf_op jit(solution)/shard_map/ppermute | solution.py:21
  94.6 1.2 %shard_map.109 = bf16[384,1024]{1,0:T(8,128)(2,1)} custom-call(bf16[384,1024]{1,0:T(8,128)(2,1)S(1)} %fusion.base_ref, f32[192,1024]{1,0:T(8,128)S(1)} %get-tuple-element.43.refs_0_, bf16[192,1024]{1,0:T(8,128)(2,1)S(1)} %collective-permute-done.10.refs_1_, bf16[192,1024]{1,0:T(8,128)(2,1)S(1)} %collective-permute-done.11.refs_2_, ...), custom_call_target="tpu_custom_call" | custom-call | bytes 3932160 | tf_op jit(solution)/shard_map/pallas_call | solution.py:365
  (82 shorter events, 0.9 us)
Async XLA Ops:
  0.0 16.6 %copy-start.21 = (s32[2]{0:T(128)S(1)}, s32[2]{0:T(128)}, u32[]{:S(2)}) copy-start(s32[2]{0:T(128)} %constant.73) | copy-start | bytes 28
  0.0 14.5 %copy-start.22 = (s32[64]{0:T(128)S(1)}, s32[64]{0:T(128)}, u32[]{:S(2)}) copy-start(s32[64]{0:T(128)} %param.13) | copy-start | bytes 772
  0.0 14.6 %copy-start.19 = (s32[64,2]{0,1:T(2,128)S(1)}, s32[64,2]{0,1:T(2,128)}, u32[]{:S(2)}) copy-start(s32[64,2]{0,1:T(2,128)} %param.12) | copy-start | bytes 1540
  0.0 15.2 %copy-start.20 = (s32[64]{0:T(128)S(1)}, s32[64]{0:T(128)}, u32[]{:S(2)}) copy-start(s32[64]{0:T(128)} %param.14) | copy-start | bytes 772
  0.0 16.6 %copy-start.18 = (bf16[1024]{0:T(1024)(128)(2,1)S(1)}, bf16[1024]{0:T(1024)(128)(2,1)}, u32[]{:S(2)}) copy-start(bf16[1024]{0:T(1024)(128)(2,1)} %param.15) | copy-start | bytes 6148
  0.0 16.6 %copy-start.17 = (bf16[4096]{0:T(1024)(128)(2,1)S(1)}, bf16[4096]{0:T(1024)(128)(2,1)}, u32[]{:S(2)}) copy-start(bf16[4096]{0:T(1024)(128)(2,1)} %param.16) | copy-start | bytes 24580
  1.3 26.1 %collective-permute-start.5 = (bf16[192,1024]{1,0:T(8,128)(2,1)S(1)}, bf16[192,1024]{1,0:T(8,128)(2,1)S(1)}, u32[]{:S(2)}, u32[]{:S(2)}) collective-permute-start(bf16[192,1024]{1,0:T(8,128)(2,1)S(1)} %get-tuple-element.52.refs_0_), channel_id=1, source_target_pairs={{0,2},{1,3},{2,0},{3,1},{4,6},{5,7},{6,4},{7,5},{8,10},{9,11},{10,... | collective-permute-start | bytes 1179656 | tf_op jit(solution)/shard_map/ppermute | solution.py:21
  4.3 24.9 %collective-permute-start.3 = (bf16[192,1024]{1,0:T(8,128)(2,1)S(1)}, bf16[192,1024]{1,0:T(8,128)(2,1)S(1)}, u32[]{:S(2)}, u32[]{:S(2)}) collective-permute-start(bf16[192,1024]{1,0:T(8,128)(2,1)S(1)} %get-tuple-element.52.refs_0_), channel_id=1, source_target_pairs={{0,1},{1,0},{2,3},{3,2},{4,5},{5,4},{6,7},{7,6},{8,9},{9,8},{10,11... | collective-permute-start | bytes 1179656 | tf_op jit(solution)/shard_map/ppermute | solution.py:21
  5.8 20.1 %collective-permute-start.4 = (bf16[192,1024]{1,0:T(8,128)(2,1)S(1)}, bf16[192,1024]{1,0:T(8,128)(2,1)S(1)}, u32[]{:S(2)}, u32[]{:S(2)}) collective-permute-start(bf16[192,1024]{1,0:T(8,128)(2,1)S(1)} %get-tuple-element.51.refs_1_), channel_id=1, source_target_pairs={{0,1},{1,0},{2,3},{3,2},{4,5},{5,4},{6,7},{7,6},{8,9},{9,8},{10,11... | collective-permute-start | bytes 1179656 | tf_op jit(solution)/shard_map/ppermute | solution.py:21
  6.3 24.4 %collective-permute-start.6 = (bf16[192,1024]{1,0:T(8,128)(2,1)S(1)}, bf16[192,1024]{1,0:T(8,128)(2,1)S(1)}, u32[]{:S(2)}, u32[]{:S(2)}) collective-permute-start(bf16[192,1024]{1,0:T(8,128)(2,1)S(1)} %get-tuple-element.51.refs_1_), channel_id=1, source_target_pairs={{0,2},{1,3},{2,0},{3,1},{4,6},{5,7},{6,4},{7,5},{8,10},{9,11},{10,... | collective-permute-start | bytes 1179656 | tf_op jit(solution)/shard_map/ppermute | solution.py:21
  7.1 1.1 %copy-start.7 = (bf16[8,6,6,1024]{3,0,2,1:T(8,128)(2,1)S(1)}, bf16[8,6,6,1024]{3,0,2,1:T(8,128)(2,1)}, u32[]{:S(2)}) copy-start(bf16[8,6,6,1024]{3,0,2,1:T(8,128)(2,1)} %param.11) | copy-start | bytes 1769476
  9.2 15.0 %all-to-all-start = ((bf16[8,16,1024]{2,1,0:T(8,128)(2,1)}), bf16[8,16,1024]{2,1,0:T(8,128)(2,1)S(1)}, u32[]{:S(2)}, u32[]{:S(2)}) async-start(bf16[8,16,1024]{2,1,0:T(8,128)(2,1)} %shard_map.100), calls=%async_computation | async-start | bytes 524288 | tf_op jit(solution)/shard_map/all_to_all | solution.py:404
  24.3 16.3 %collective-permute-start = (bf16[80,1024]{1,0:T(8,128)(2,1)S(1)}, bf16[80,1024]{1,0:T(8,128)(2,1)S(1)}, u32[]{:S(2)}, u32[]{:S(2)}) collective-permute-start(bf16[80,1024]{1,0:T(8,128)(2,1)S(1)} %shard_map.101.refs_0_), channel_id=1, source_target_pairs={{0,1},{1,0},{2,3},{3,2},{4,5},{5,4},{6,7},{7,6},{8,9},{9,8},{10,11... | collective-permute-start | bytes 491528 | tf_op jit(solution)/shard_map/ppermute | solution.py:21
  25.9 14.7 %collective-permute-start.1 = (bf16[80,1024]{1,0:T(8,128)(2,1)S(1)}, bf16[80,1024]{1,0:T(8,128)(2,1)S(1)}, u32[]{:S(2)}, u32[]{:S(2)}) collective-permute-start(bf16[80,1024]{1,0:T(8,128)(2,1)S(1)} %shard_map.101.refs_0_), channel_id=1, source_target_pairs={{0,2},{1,3},{2,0},{3,1},{4,6},{5,7},{6,4},{7,5},{8,10},{9,11},{10,... | collective-permute-start | bytes 491528 | tf_op jit(solution)/shard_map/ppermute | solution.py:21
  27.4 13.2 %collective-permute-start.2 = (bf16[80,1024]{1,0:T(8,128)(2,1)S(1)}, bf16[80,1024]{1,0:T(8,128)(2,1)S(1)}, u32[]{:S(2)}, u32[]{:S(2)}) collective-permute-start(bf16[80,1024]{1,0:T(8,128)(2,1)S(1)} %shard_map.101.refs_0_), channel_id=1, source_target_pairs={{0,3},{1,2},{2,1},{3,0},{4,7},{5,6},{6,5},{7,4},{8,11},{9,10},{10,... | collective-permute-start | bytes 491528 | tf_op jit(solution)/shard_map/ppermute | solution.py:21
  29.2 27.7 %collective-permute-start.7 = (bf16[192,1024]{1,0:T(8,128)(2,1)S(1)}, bf16[192,1024]{1,0:T(8,128)(2,1)S(1)}, u32[]{:S(2)}, u32[]{:S(2)}) collective-permute-start(bf16[192,1024]{1,0:T(8,128)(2,1)S(1)} %collective-permute-done.5.refs_2_), channel_id=1, source_target_pairs={{0,1},{1,0},{2,3},{3,2},{4,5},{5,4},{6,7},{7,6},{8,9},{9,8},{10,11... | collective-permute-start | bytes 1179656 | tf_op jit(solution)/shard_map/ppermute | solution.py:21
  30.7 8.4 %copy-start.8 = (bf16[192,1024]{1,0:T(8,128)(2,1)}, bf16[192,1024]{1,0:T(8,128)(2,1)S(1)}, u32[]{:S(2)}) copy-start(bf16[192,1024]{1,0:T(8,128)(2,1)S(1)} %collective-permute-done.6.refs_3_) | copy-start | bytes 1179652
  30.7 26.9 %collective-permute-start.8 = (bf16[192,1024]{1,0:T(8,128)(2,1)S(1)}, bf16[192,1024]{1,0:T(8,128)(2,1)}, u32[]{:S(2)}, u32[]{:S(2)}) collective-permute-start(bf16[192,1024]{1,0:T(8,128)(2,1)S(1)} %collective-permute-done.4.refs_1_), channel_id=1, source_target_pairs={{0,2},{1,3},{2,0},{3,1},{4,6},{5,7},{6,4},{7,5},{8,10},{9,11},{10,... | collective-permute-start | bytes 1179656 | tf_op jit(solution)/shard_map/ppermute | solution.py:21
  32.3 4.6 %copy-start = (bf16[4096,3,512]{2,0,1:T(8,128)(2,1)S(1)}, bf16[4096,3,512]{2,0,1:T(8,128)(2,1)}, u32[]{:S(2)}) copy-start(bf16[4096,3,512]{2,0,1:T(8,128)(2,1)} %param.17) | copy-start | bytes 37748740
  36.8 5.5 %copy-start.1 = (bf16[4096,3,512]{2,0,1:T(8,128)(2,1)S(1)}, bf16[4096,3,512]{2,0,1:T(8,128)(2,1)}, u32[]{:S(2)}) copy-start(bf16[4096,3,512]{2,0,1:T(8,128)(2,1)} %param.17) | copy-start | bytes 37748740
  39.2 1.4 %copy-start.5 = (f32[3,384,512]{2,1,0:T(8,128)}, f32[3,384,512]{2,1,0:T(8,128)S(1)}, u32[]{:S(2)}) copy-start(f32[3,384,512]{2,1,0:T(8,128)S(1)} %get-tuple-element.37.refs_6_) | copy-start | bytes 7077892
  40.6 8.2 %copy-start.9 = (bf16[192,1024]{1,0:T(8,128)(2,1)S(1)}, bf16[192,1024]{1,0:T(8,128)(2,1)}, u32[]{:S(2)}) copy-start(bf16[192,1024]{1,0:T(8,128)(2,1)} %copy-done.8) | copy-start | bytes 1179652
  40.6 0.7 copy-start.14
  42.3 0.9 copy-start.15
  43.2 14.5 %slice-start = ((s8[12582912]{0:T(1024)(128)(4,1)}), s8[4194304]{0:T(1024)(128)(4,1)S(1)}, s32[]{:S(2)}) async-start(s8[12582912]{0:T(1024)(128)(4,1)} %bitcast.27), calls=%async_computation.1 | async-start | bytes 8388608
  43.2 14.5 %slice-start.1 = ((s8[12582912]{0:T(1024)(128)(4,1)}), s8[4194304]{0:T(1024)(128)(4,1)S(1)}, s32[]{:S(2)}) async-start(s8[12582912]{0:T(1024)(128)(4,1)} %bitcast.27), calls=%async_computation.2 | async-start | bytes 8388608
  48.1 0.7 copy-start.12
  48.8 1.7 %copy-start.6 = (f32[3,384,512]{2,1,0:T(8,128)S(1)}, f32[3,384,512]{2,1,0:T(8,128)}, u32[]{:S(2)}) copy-start(f32[3,384,512]{2,1,0:T(8,128)} %copy-done.5) | copy-start | bytes 7077892
  50.5 7.3 %slice-start.2 = ((s8[12582912]{0:T(1024)(128)(4,1)}), s8[4194304]{0:T(1024)(128)(4,1)S(1)}, s32[]{:S(2)}) async-start(s8[12582912]{0:T(1024)(128)(4,1)} %bitcast.27), calls=%async_computation.3 | async-start | bytes 8388608
  50.5 7.3 %copy-start.2 = (bf16[512,4096]{1,0:T(8,128)(2,1)S(1)}, bf16[512,4096]{1,0:T(8,128)(2,1)}, u32[]{:S(2)}) copy-start(bf16[512,4096]{1,0:T(8,128)(2,1)} %w_ref.5) | copy-start | bytes 12582916
  55.4 1.4 %copy-start.3 = (f32[3,384,512]{2,1,0:T(8,128)}, f32[3,384,512]{2,1,0:T(8,128)S(1)}, u32[]{:S(2)}) copy-start(f32[3,384,512]{2,1,0:T(8,128)S(1)} %get-tuple-element.39.acc_ref) | copy-start | bytes 7077892
  56.9 0.7 copy-start.10
  57.8 1.7 %copy-start.4 = (f32[3,384,512]{2,1,0:T(8,128)S(1)}, f32[3,384,512]{2,1,0:T(8,128)}, u32[]{:S(2)}) copy-start(f32[3,384,512]{2,1,0:T(8,128)} %copy-done.3) | copy-start | bytes 7077892
  59.4 1.0 %copy-start.11 = (bf16[192,1024]{1,0:T(8,128)(2,1)S(1)}, bf16[192,1024]{1,0:T(8,128)(2,1)}, u32[]{:S(2)}) copy-start(bf16[192,1024]{1,0:T(8,128)(2,1)} %copy-done.10) | copy-start | bytes 1179652
  68.4 12.1 %collective-permute-start.13 = (bf16[192,1024]{1,0:T(8,128)(2,1)S(1)}, bf16[192,1024]{1,0:T(8,128)(2,1)S(1)}, u32[]{:S(2)}, u32[]{:S(2)}) collective-permute-start(bf16[192,1024]{1,0:T(8,128)(2,1)S(1)} %get-tuple-element.50), channel_id=1, source_target_pairs={{0,2},{1,3},{2,0},{3,1},{4,6},{5,7},{6,4},{7,5},{8,10},{9,11},{10,... | collective-permute-start | bytes 1179656 | tf_op jit(solution)/shard_map/ppermute | solution.py:21
  69.0 12.3 %collective-permute-start.9 = (bf16[192,1024]{1,0:T(8,128)(2,1)S(1)}, bf16[192,1024]{1,0:T(8,128)(2,1)S(1)}, u32[]{:S(2)}, u32[]{:S(2)}) collective-permute-start(bf16[192,1024]{1,0:T(8,128)(2,1)S(1)} %get-tuple-element.45), channel_id=1, source_target_pairs={{0,1},{1,0},{2,3},{3,2},{4,5},{5,4},{6,7},{7,6},{8,9},{9,8},{10,11... | collective-permute-start | bytes 1179656 | tf_op jit(solution)/shard_map/ppermute | solution.py:21
  70.4 12.3 %copy-start.13 = (bf16[80,1024]{1,0:T(8,128)(2,1)S(1)}, bf16[80,1024]{1,0:T(8,128)(2,1)}, u32[]{:S(2)}) copy-start(bf16[80,1024]{1,0:T(8,128)(2,1)} %copy-done.12) | copy-start | bytes 491524
  70.4 12.3 %copy-start.16 = (bf16[384,1024]{1,0:T(8,128)(2,1)S(1)}, bf16[384,1024]{1,0:T(8,128)(2,1)}, u32[]{:S(2)}) copy-start(bf16[384,1024]{1,0:T(8,128)(2,1)} %param.10) | copy-start | bytes 2359300
  70.5 19.0 %collective-permute-start.11 = (bf16[192,1024]{1,0:T(8,128)(2,1)S(1)}, bf16[192,1024]{1,0:T(8,128)(2,1)S(1)}, u32[]{:S(2)}, u32[]{:S(2)}) collective-permute-start(bf16[192,1024]{1,0:T(8,128)(2,1)S(1)} %get-tuple-element.46), channel_id=1, source_target_pairs={{0,1},{1,0},{2,3},{3,2},{4,5},{5,4},{6,7},{7,6},{8,9},{9,8},{10,11... | collective-permute-start | bytes 1179656 | tf_op jit(solution)/shard_map/ppermute | solution.py:21
  72.8 16.7 %collective-permute-start.12 = (bf16[192,1024]{1,0:T(8,128)(2,1)S(1)}, bf16[192,1024]{1,0:T(8,128)(2,1)S(1)}, u32[]{:S(2)}, u32[]{:S(2)}) collective-permute-start(bf16[192,1024]{1,0:T(8,128)(2,1)S(1)} %get-tuple-element.48), channel_id=1, source_target_pairs={{0,2},{1,3},{2,0},{3,1},{4,6},{5,7},{6,4},{7,5},{8,10},{9,11},{10,... | collective-permute-start | bytes 1179656 | tf_op jit(solution)/shard_map/ppermute | solution.py:21
  80.7 14.0 %collective-permute-start.14 = (bf16[192,1024]{1,0:T(8,128)(2,1)S(1)}, bf16[192,1024]{1,0:T(8,128)(2,1)S(1)}, u32[]{:S(2)}, u32[]{:S(2)}) collective-permute-start(bf16[192,1024]{1,0:T(8,128)(2,1)S(1)} %add_convert_fusion), channel_id=1, source_target_pairs={{0,1},{1,0},{2,3},{3,2},{4,5},{5,4},{6,7},{7,6},{8,9},{9,8},{10,11... | collective-permute-start | bytes 1179656 | tf_op jit(solution)/shard_map/ppermute | solution.py:21
  81.4 13.2 %collective-permute-start.10 = (bf16[192,1024]{1,0:T(8,128)(2,1)S(1)}, bf16[192,1024]{1,0:T(8,128)(2,1)S(1)}, u32[]{:S(2)}, u32[]{:S(2)}) collective-permute-start(bf16[192,1024]{1,0:T(8,128)(2,1)S(1)} %add_convert_fusion.1), channel_id=1, source_target_pairs={{0,2},{1,3},{2,0},{3,1},{4,6},{5,7},{6,4},{7,5},{8,10},{9,11},{10,... | collective-permute-start | bytes 1179656 | tf_op jit(solution)/shard_map/ppermute | solution.py:21

commit v2 on v1

v2 whole, which is shorter than its diff:
```python
import functools

import jax
import jax.numpy as jnp
from jax import lax
from jax.experimental import pallas as pl
from jax.experimental.pallas import tpu as pltpu
from jax.sharding import PartitionSpec as P

D = 4096
HD = 128
EPS = 1e-05
LOG2E = 1.4426950408889634
TINY = pl.CostEstimate(flops=0, bytes_accessed=0, transcendentals=0)


def round_up(n, m):
    return -(-n // m) * m


def swap(x, s):
    n = lax.axis_size("tensor")
    return lax.ppermute(x, "tensor", [(i, i ^ s) for i in range(n)])


def low_bit(s):
    return s & -s


def high_bit(s):
    return 1 << (s.bit_length() - 1)


def by_bits(n, reverse=False):
    return sorted(range(1, n), key=lambda s: (bin(s).count("1"), s), reverse=reverse)


def gather_halves(top, bottom, n):
    blocks = {0: (top, bottom)}
    for s in by_bits(n):
        low, high = low_bit(s), high_bit(s)
        if low == high:
            other = (swap(top, s), swap(bottom, s))
        else:
            other = (swap(blocks[s ^ low][0], low), swap(blocks[s ^ high][1], high))
        blocks[s] = other
    return blocks


def vmem_specs(n):
    return [pl.BlockSpec(memory_space=pltpu.VMEM)] * n


def params(mib):
    return pltpu.CompilerParams(vmem_limit_bytes=mib * 1024 * 1024)


def pool_kernel(me_ref, map_ref, x_ref, out_ref, tmp_ref):
    n_req, region = out_ref.shape[0], tmp_ref.shape[1]
    side, img_dev = x_ref.shape[0], x_ref.shape[2]
    half = side // 2
    rows = lax.broadcasted_iota(jnp.int32, (n_req, img_dev), 0)
    onehot = (rows == map_ref[pl.ds(me_ref[0], 1), :]).astype(jnp.bfloat16)
    tmp_ref[...] = jnp.zeros_like(tmp_ref)
    for i in range(half):
        for j in range(half):
            total = x_ref[2 * i, 2 * j].astype(jnp.float32)
            for a, b in ((0, 1), (1, 0), (1, 1)):
                total += x_ref[2 * i + a, 2 * j + b].astype(jnp.float32)
            pooled = (total * 0.25).astype(jnp.bfloat16)
            tmp_ref[:, i * half + j, :] = jnp.dot(onehot, pooled, preferred_element_type=jnp.float32)
    out_ref[...] = tmp_ref[...].astype(jnp.bfloat16)


def pool_images(me, req_map, patches):
    n_req = req_map.shape[0]
    side, _, img_dev, width = patches.shape
    padded = round_up((side // 2) ** 2, 16)
    return pl.pallas_call(
        pool_kernel,
        out_shape=jax.ShapeDtypeStruct((n_req, padded, width), jnp.bfloat16),
        in_specs=[pl.BlockSpec(memory_space=pltpu.SMEM)] + vmem_specs(2),
        out_specs=pl.BlockSpec(memory_space=pltpu.VMEM),
        scratch_shapes=[pltpu.VMEM((n_req, padded, width), jnp.float32)],
        compiler_params=params(24),
        cost_estimate=TINY,
    )(me[None], req_map, patches)


def pack_kernel(region, rec_ref, gain_ref, out_ref, tmp_ref):
    n_req = rec_ref.shape[0]
    for r in range(n_req):
        tmp_ref[region * r : region * (r + 1)] = rec_ref[r].astype(jnp.float32)[:region]
    rest = tmp_ref.shape[0] - region * n_req
    tmp_ref[region * n_req :] = jnp.broadcast_to(gain_ref[0:1, :], (rest, gain_ref.shape[1]))
    out_ref[...] = tmp_ref[...].astype(jnp.bfloat16)


def pack_images(received, gain, region, n_img):
    width = received.shape[2]
    return pl.pallas_call(
        functools.partial(pack_kernel, region),
        out_shape=jax.ShapeDtypeStruct((n_img, width), jnp.bfloat16),
        in_specs=vmem_specs(2),
        out_specs=pl.BlockSpec(memory_space=pltpu.VMEM),
        scratch_shapes=[pltpu.VMEM((n_img, width), jnp.float32)],
        compiler_params=params(24),
        cost_estimate=TINY,
    )(received, gain)


def load_kernel(qkv_ref, out_ref, qkv_vmem, out_vmem, sem_ref):
    copies = [
        pltpu.make_async_copy(qkv_ref, qkv_vmem, sem_ref.at[0]),
        pltpu.make_async_copy(out_ref, out_vmem, sem_ref.at[1]),
    ]
    for copy in copies:
        copy.start()
    for copy in copies:
        copy.wait()


def load_weights(w_qkv, w_out):
    return pl.pallas_call(
        load_kernel,
        out_shape=(pltpu.VMEM(w_qkv.shape, w_qkv.dtype), pltpu.VMEM(w_out.shape, w_out.dtype)),
        in_specs=[pl.BlockSpec(memory_space=pltpu.HBM)] * 2,
        out_specs=tuple(vmem_specs(2)),
        scratch_shapes=[pltpu.SemaphoreType.DMA((2,))],
        compiler_params=params(4),
        cost_estimate=TINY,
    )(w_qkv, w_out)


def cols_of(ref, owner, width):
    return ref[:, pl.ds(pl.multiple_of(owner * width, width), width)]


def rows_of(ref, j, owner, width):
    return ref[j, pl.ds(pl.multiple_of(owner * width, width), width)]


def text_kernel(n_blk, has_acc, idx_ref, *refs):
    x_refs, refs = refs[: 2 * n_blk], refs[2 * n_blk :]
    if has_acc:
        gain_ref, w_ref, acc_in, ss_in, acc_ref, ss_ref = refs
    else:
        gain_ref, w_ref, acc_ref, ss_ref = refs
    half, width = x_refs[0].shape
    scaled = []
    for side in range(2):
        rows = pl.ds(side * half, half)
        total = ss_in[rows] if has_acc else jnp.zeros((half, 128), jnp.float32)
        for s in range(n_blk):
            xf = x_refs[2 * s + side][...].astype(jnp.float32)
            scaled.append((xf * gain_ref[idx_ref[s]]).astype(jnp.bfloat16))
            total += jnp.sum(xf * xf, axis=1, keepdims=True)
        ss_ref[rows] = total
    for s in range(n_blk):
        for j in range(3):
            weight = rows_of(w_ref, j, idx_ref[s], width)
            for side in range(2):
                rows = pl.ds(side * half, half)
                prod = jnp.dot(scaled[side * n_blk + s], weight, preferred_element_type=jnp.float32)
                if s > 0:
                    prod += acc_ref[j, rows]
                elif has_acc:
                    prod += acc_in[j, rows]
                acc_ref[j, rows] = prod


def text_part(idx, blocks, gain, w, acc=None, ss=None):
    n_blk = len(blocks)
    half, width = blocks[0][0].shape
    rows, cols = 2 * half, w.shape[2]
    has_acc = acc is not None
    args = [h for b in blocks for h in b] + [gain, w]
    in_specs = vmem_specs(2 * n_blk + 2)
    if has_acc:
        args += [acc, ss]
        in_specs += vmem_specs(2)
    return pl.pallas_call(
        functools.partial(text_kernel, n_blk, has_acc),
        out_shape=(
            jax.ShapeDtypeStruct((3, rows, cols), jnp.float32),
            jax.ShapeDtypeStruct((rows, 128), jnp.float32),
        ),
        in_specs=[pl.BlockSpec(memory_space=pltpu.SMEM)] + in_specs,
        out_specs=tuple(vmem_specs(2)),
        compiler_params=params(16),
        cost_estimate=TINY,
    )(idx, *args)


def image_kernel(n_blk, n_rows, idx_ref, *refs):
    x_refs, (gain_ref, w_ref, qkv_ref, own_ref) = refs[:n_blk], refs[n_blk:]
    width = gain_ref.shape[2]
    total = 0.0
    for s in range(n_blk):
        xf = x_refs[s][...].astype(jnp.float32)
        total += jnp.sum(xf * xf, axis=1, keepdims=True)
    scale = lax.rsqrt(total / D + EPS)
    total = 0.0
    scaled = []
    for s in range(n_blk):
        xf = x_refs[s][...].astype(jnp.float32)
        merged = (xf * scale * xf[n_rows : n_rows + 1]).astype(jnp.bfloat16)
        if s == 0:
            own_ref[...] = merged
        mf = merged.astype(jnp.float32)
        total += jnp.sum(mf * mf, axis=1, keepdims=True)
        scaled.append((mf * gain_ref[idx_ref[s]]).astype(jnp.bfloat16))
    scale = lax.rsqrt(total / D + EPS)
    for j in range(3):
        acc = 0.0
        for s in range(n_blk):
            weight = rows_of(w_ref, j, idx_ref[s], width)
            acc += jnp.dot(scaled[s], weight, preferred_element_type=jnp.float32)
        qkv_ref[j] = (acc * scale).astype(jnp.bfloat16)


def image_part(idx, blocks, gain, w, n_rows):
    n_blk = len(blocks)
    n_img, width = blocks[0].shape
    cols = w.shape[2]
    return pl.pallas_call(
        functools.partial(image_kernel, n_blk, n_rows),
        out_shape=(
            jax.ShapeDtypeStruct((3, n_img, cols), jnp.bfloat16),
            jax.ShapeDtypeStruct((n_img, width), jnp.bfloat16),
        ),
        in_specs=[pl.BlockSpec(memory_space=pltpu.SMEM)]
        + vmem_specs(n_blk + 2),
        out_specs=tuple(vmem_specs(2)),
        compiler_params=params(16),
        cost_estimate=TINY,
    )(idx, *blocks, gain, w)


def final_kernel(idx_ref, top_ref, bottom_ref, gain_ref, w_ref, acc_ref, ss_ref, img_ref, place_ref, text_row_ref,
                 key_ref, w_out_ref, ctx_ref, far_top_ref, far_bottom_ref, qkv_ref):
    half, width = top_ref.shape
    rows, cols = 2 * half, ctx_ref.shape[1]
    owner = idx_ref[0]
    scaled, scales = [], []
    for side, x_ref in enumerate((top_ref, bottom_ref)):
        part = pl.ds(side * half, half)
        xf = x_ref[...].astype(jnp.float32)
        scaled.append((xf * gain_ref[owner]).astype(jnp.bfloat16))
        total = ss_ref[part] + jnp.sum(xf * xf, axis=1, keepdims=True)
        scales.append((lax.rsqrt(total / D + EPS) * text_row_ref[part])[:, :1])
    for j in range(3):
        weight = rows_of(w_ref, j, owner, width)
        for side in range(2):
            part = pl.ds(side * half, half)
            prod = jnp.dot(scaled[side], weight, preferred_element_type=jnp.float32)
            put = jnp.dot(place_ref[part], img_ref[j], preferred_element_type=jnp.float32)
            qkv_ref[j, part] = ((prod + acc_ref[j, part]) * scales[side] + put).astype(jnp.bfloat16)
    step = 128
    heads = [pl.ds(h * HD, HD) for h in range(cols // HD)]
    for r in range(rows // step):
        here, last = pl.ds(r * step, step), (r + 1) * step
        row = lax.broadcasted_iota(jnp.int32, (step, last), 0) + r * step
        col = lax.broadcasted_iota(jnp.int32, (step, last), 1)
        bias = jnp.where((row >= col) & (key_ref[0:1, pl.ds(0, last)] > 0.5), 0.0, -1e30)
        scores = [
            lax.dot_general(
                qkv_ref[0, here, lanes],
                qkv_ref[1, pl.ds(0, last), lanes],
                (((1,), (1,)), ((), ())),
                preferred_element_type=jnp.float32,
            )
            for lanes in heads
        ]
        scores = [x * (LOG2E / HD**0.5) + bias for x in scores]
        tops = [jnp.max(x, axis=1, keepdims=True) for x in scores]
        expo = [jnp.exp2(x - top) for x, top in zip(scores, tops)]
        sums = [jnp.sum(x, axis=1, keepdims=True) for x in expo]
        outs = [
            jnp.dot(x.astype(jnp.bfloat16), qkv_ref[2, pl.ds(0, last), lanes], preferred_element_type=jnp.float32)
            for x, lanes in zip(expo, heads)
        ]
        for lanes, out, total in zip(heads, outs, sums):
            ctx_ref[here, lanes] = (out / total).astype(jnp.bfloat16)
    weight = cols_of(w_out_ref, owner, width)
    for side, out_ref in enumerate((far_top_ref, far_bottom_ref)):
        out_ref[...] = jnp.dot(
            ctx_ref[pl.ds(side * half, half)], weight, preferred_element_type=jnp.float32
        ).astype(jnp.bfloat16)


def final_part(idx, block, gain, w, acc, ss, img, place, text_row, key_ok, w_out):
    half, width = block[0].shape
    rows, cols = 2 * half, w.shape[2]
    return pl.pallas_call(
        final_kernel,
        out_shape=(
            jax.ShapeDtypeStruct((rows, cols), jnp.bfloat16),
            jax.ShapeDtypeStruct((half, width), jnp.bfloat16),
            jax.ShapeDtypeStruct((half, width), jnp.bfloat16),
        ),
        in_specs=[pl.BlockSpec(memory_space=pltpu.SMEM)]
        + vmem_specs(11),
        out_specs=tuple(vmem_specs(3)),
        scratch_shapes=[pltpu.VMEM((3, rows, cols), jnp.bfloat16)],
        compiler_params=params(16),
        cost_estimate=TINY,
    )(idx, *block, gain, w, acc, ss, img, place, text_row, key_ok, w_out)


def out_kernel(idx_ref, ctx_ref, w_ref, top_ref, bottom_ref):
    half, width = top_ref.shape
    weight = cols_of(w_ref, idx_ref[0], width)
    for side, out_ref in enumerate((top_ref, bottom_ref)):
        out_ref[...] = jnp.dot(
            ctx_ref[pl.ds(side * half, half)], weight, preferred_element_type=jnp.float32
        ).astype(out_ref.dtype)


def out_part(idx, ctx, w, width, dtype=jnp.bfloat16):
    rows, depth = ctx.shape
    return pl.pallas_call(
        out_kernel,
        out_shape=(
            jax.ShapeDtypeStruct((rows // 2, width), dtype),
            jax.ShapeDtypeStruct((rows // 2, width), dtype),
        ),
        in_specs=[pl.BlockSpec(memory_space=pltpu.SMEM)] + vmem_specs(2),
        out_specs=tuple(vmem_specs(2)),
        compiler_params=params(16),
        cost_estimate=TINY,
    )(idx, ctx, w)


def add_kernel(n_top, base_ref, *refs):
    out_ref = refs[-1]
    half = out_ref.shape[0] // 2
    for side, terms in enumerate((refs[:n_top], refs[n_top:-1])):
        part = pl.ds(side * half, half)
        total = terms[0][...].astype(jnp.float32)
        for term in terms[1:]:
            total += term[...].astype(jnp.float32)
        out_ref[part] = (base_ref[part].astype(jnp.float32) + total).astype(out_ref.dtype)


def add_all(base, top, bottom):
    return pl.pallas_call(
        functools.partial(add_kernel, len(top)),
        out_shape=jax.ShapeDtypeStruct(base.shape, jnp.bfloat16),
        in_specs=vmem_specs(1 + len(top) + len(bottom)),
        out_specs=pl.BlockSpec(memory_space=pltpu.VMEM),
        compiler_params=params(16),
        cost_estimate=pl.CostEstimate(
            flops=0, bytes_accessed=2 * base.size * (2 + len(top)), transcendentals=0
        ),
    )(base, *top, *bottom)


def scatter_terms(parts, n):
    acc = {s: [[parts[s][0]], [parts[s][1]]] for s in range(n)}
    for s in by_bits(n, reverse=True):
        for side, bit in ((0, low_bit(s)), (1, high_bit(s))):
            terms = [t.astype(jnp.float32) for t in acc[s][side]]
            out = functools.reduce(lambda a, b: a + b, terms).astype(jnp.bfloat16)
            acc[s ^ bit][side].append(swap(out, bit))
    return acc[0]


def body(text, patches, grids, image_request, slot_start, vis_gain, dec_gain, w_qkv, w_out):
    n_req = lax.axis_size("req")
    n_ten = lax.axis_size("tensor")
    me_req = lax.axis_index("req")
    me_ten = lax.axis_index("tensor")
    img_dev, side, _, width = patches.shape
    half = side // 2
    region = half * half
    length = text.shape[0]
    w3 = jnp.transpose(w_qkv, (1, 0, 2))
    owners = [(me_ten ^ s).astype(jnp.int32) for s in range(n_ten)]
    gains = dec_gain.astype(jnp.float32).reshape(n_ten, 1, width)

    blocks = gather_halves(text[: length // 2], text[length // 2 :], n_ten)

    req_map = image_request.reshape(n_req, img_dev)
    outgoing = pool_images(me_req.astype(jnp.int32), req_map, jnp.transpose(patches, (1, 2, 0, 3)))
    w3, w_out, outgoing = lax.optimization_barrier((w3, w_out, outgoing))
    w3, w_out = load_weights(w3, w_out)
    received = lax.all_to_all(outgoing, "req", split_axis=0, concat_axis=0, tiled=True)
    n_rows = n_req * region
    n_img = round_up(n_rows + 1, 16)
    img_own = pack_images(received, vis_gain.astype(jnp.float32).reshape(1, width), region, n_img)
    img_blocks = [img_own] + [swap(img_own, s) for s in range(1, n_ten)]
    near = [blocks[s] for s in by_bits(n_ten)[:-1]]
    img_blocks, near = lax.optimization_barrier((img_blocks, near))
    img_qkv, merged = image_part(jnp.stack(owners), img_blocks, gains, w3, n_rows)

    pick = req_map == me_req
    has_img = jnp.any(pick, axis=1)
    start_src = jnp.sum(jnp.where(pick, slot_start.reshape(n_req, img_dev), 0), axis=1)
    grid_src = jnp.sum(jnp.where(pick[:, :, None], grids.reshape(n_req, img_dev, 2), 0), axis=1)
    cells = jnp.arange(region, dtype=jnp.int32)
    row_i = cells // half
    col_j = cells % half
    height = grid_src[:, 0][:, None] // 2
    grid_w = grid_src[:, 1][:, None] // 2
    valid = has_img[:, None] & (row_i[None, :] < height) & (col_j[None, :] < grid_w)
    pos = jnp.where(valid, start_src[:, None] + row_i[None, :] * grid_w + col_j[None, :], -1)
    rpos = jnp.where(has_img[:, None], start_src[:, None] + cells[None, :], -1)
    pos = jnp.pad(pos.reshape(-1), (0, n_img - n_rows), constant_values=-1)
    spots = jnp.arange(length, dtype=jnp.int32)
    hit = spots[:, None] == pos[None, :]
    place = hit.astype(jnp.bfloat16)
    is_img = jnp.any(hit, axis=1)
    in_region = jnp.any(rpos.reshape(-1)[:, None] == spots[None, :], axis=0)
    is_key = jnp.any(pos[:, None] == spots[None, :], axis=0)
    key_ok = jnp.broadcast_to((~in_region | is_key).astype(jnp.float32)[None, :], (8, length))
    text_row = jnp.broadcast_to(1.0 - is_img.astype(jnp.float32)[:, None], (length, 128))
    img_here = jnp.dot(place, merged, preferred_element_type=jnp.float32).astype(jnp.bfloat16)
    x_in = jnp.where(is_img[:, None], img_here, text)

    order = by_bits(n_ten)
    acc, ss = text_part(owners[0][None], [blocks[0]], gains, w3)
    acc, ss = text_part(jnp.stack([owners[s] for s in order[:-1]]), near, gains, w3, acc, ss)
    far = order[-1]
    context, far_top, far_bottom = final_part(
        owners[far][None], blocks[far], gains, w3, acc, ss, img_qkv, place, text_row, key_ok, w_out
    )
    parts = {far: (far_top, far_bottom)}
    for s in reversed([0] + order[:-1]):
        parts[s] = out_part(owners[s][None], context, w_out, width, jnp.float32 if s == 0 else jnp.bfloat16)
    top, bottom = scatter_terms(parts, n_ten)
    return add_all(x_in, top, bottom)


def solution(mesh):
    in_specs = (
        P("req", "tensor"),
        P("req", None, None, "tensor"),
        P(),
        P(),
        P(),
        P("tensor"),
        P(),
        P(None, None, "tensor"),
        P("tensor", None),
    )
    out_specs = P("req", "tensor")
    return jax.shard_map(body, mesh=mesh, in_specs=in_specs, out_specs=out_specs, check_vma=False)
```

time: 96.4 us -> 80.4 us (0.83)
  local copies, waits for them, and re-layouts: 21.9 us -> 13.8 us
  Pallas kernels: 24.8 us -> 17.6 us
  other arithmetic: 1.26 us -> 2.6 us
  starting transfers between devices: 23.3 us -> 22 us
    unnamed x52 -> x12, local copies, waits for them, and re-layouts: 16.9 us -> 9.42 us
    all_to_all x1, waiting for transfers between devices: 6.98 us -> 0.01 us  [body(): lax.all_to_all(outgoing, 'req', split_axis=0, concat_axis=0, tiled=True)]
    ppermute x15, waiting for transfers between devices: 16.9 us -> 23.2 us  [swap(): return lax.ppermute(x, 'tensor', [(i, i ^ s) for i in range(n)])]
    pallas_call x1, Pallas kernels: 7.95 us -> 4.23 us  [final_part(): pl.pallas_call(final_kernel, out_shape=(jax.ShapeDtypeStruct((rows, cols)...]
    pallas_call x2, Pallas kernels: 7.26 us -> 4.71 us  [text_part(): pl.pallas_call(functools.partial(text_kernel, n_blk, has_acc), out_shape=...]
    gather x5 -> x0, local copies, waits for them, and re-layouts: 1.78 us -> none  [the longest x3 1.21 us: body(): acc, ss = text_part(owners[near_at], near, gains[near_at], w3, acc, ss)]
    pallas_call x1, Pallas kernels: 4.88 us -> 3.49 us  [image_part(): pl.pallas_call(functools.partial(image_kernel, n_blk, n_rows), out_shape=...]
    ppermute x15, starting transfers between devices: 18 us -> 16.7 us  [swap(): return lax.ppermute(x, 'tensor', [(i, i ^ s) for i in range(n)])]
  transfers between devices with their start and end apart: 16 -> 16, of which waited for: 4 -> 5; matrix products, arithmetic and copies ran while one was open for 5% -> 8% of each run, Pallas kernels for 16% -> 15%
where the time goes in v2:
time: 80.4 us; the launch traced here: 79.8 us
  waiting for transfers between devices  23.2 us (29%)
  starting transfers between devices  22 us (27%)
  Pallas kernels  17.6 us (22%)
  local copies, waits for them, and re-layouts  13.8 us (17%)
  other arithmetic  2.6 us (3%)
    ppermute x15, waiting for transfers between devices, swap(): return lax.ppermute(x, 'tensor', [(i, i ^ s) for i in range(n)])  23.2 us
    ppermute x15, starting transfers between devices, swap(): return lax.ppermute(x, 'tensor', [(i, i ^ s) for i in range(n)])  16.7 us
    unnamed x12, local copies, waits for them, and re-layouts  9.42 us
    all_to_all x1, starting transfers between devices, body(): lax.all_to_all(outgoing, 'req', split_axis=0, concat_axis=0, tiled=True)  5.31 us
    pallas_call x2, Pallas kernels, text_part(): pl.pallas_call(functools.partial(text_kernel, n_blk, has_acc), out_shape=...  4.71 us
    pallas_call x1, Pallas kernels, final_part(): pl.pallas_call(final_kernel, out_shape=(jax.ShapeDtypeStruct((rows, cols)...  4.23 us
    pallas_call x1, Pallas kernels, image_part(): pl.pallas_call(functools.partial(image_kernel, n_blk, n_rows), out_shape=...  3.49 us
    pallas_call x3, Pallas kernels, out_part(): pl.pallas_call(out_kernel, out_shape=(jax.ShapeDtypeStruct((rows // 2, wi...  1.8 us
  transfers between devices with their start and end apart: 16, of which 5 were waited for; matrix products, arithmetic and copies ran while one was open for 8% of the time, Pallas kernels for 15%

profile of v2, /device:TPU:0, one launch (start us, length us, event | category | flops | bytes accessed | tf_op | source)
XLA Modules:
  0.0 79.8 jit_solution(6611793190732426449)
XLA Ops:
  0.0 1.2 %fusion.8 = (bf16[192,1024]{1,0:T(8,128)(2,1)S(1)}, bf16[192,1024]{1,0:T(8,128)(2,1)S(1)}) fusion(bf16[384,1024]{1,0:T(8,128)(2,1)} %param.9), kind=kLoop, calls=%fused_computation.36 | loop fusion | bytes 1572864 | tf_op jit(solution)/shard_map/slice | solution.py:382
  1.2 3.0 %collective-permute-start.5 = (bf16[192,1024]{1,0:T(8,128)(2,1)S(1)}, bf16[192,1024]{1,0:T(8,128)(2,1)S(1)}, u32[]{:S(2)}, u32[]{:S(2)}) collective-permute-start(bf16[192,1024]{1,0:T(8,128)(2,1)S(1)} %get-tuple-element.64.refs_0_), channel_id=1, source_target_pairs={{0,2},{1,3},{2,0},{3,1},{4,6},{5,7},{6,4},{7,5},{8,10},{9,11},{10,... | collective-permute-start | bytes 1179656 | tf_op jit(solution)/shard_map/ppermute | solution.py:23
  4.2 1.5 %collective-permute-start.3 = (bf16[192,1024]{1,0:T(8,128)(2,1)S(1)}, bf16[192,1024]{1,0:T(8,128)(2,1)S(1)}, u32[]{:S(2)}, u32[]{:S(2)}) collective-permute-start(bf16[192,1024]{1,0:T(8,128)(2,1)S(1)} %get-tuple-element.64.refs_0_), channel_id=1, source_target_pairs={{0,1},{1,0},{2,3},{3,2},{4,5},{5,4},{6,7},{7,6},{8,9},{9,8},{10,11... | collective-permute-start | bytes 1179656 | tf_op jit(solution)/shard_map/ppermute | solution.py:23
  5.7 0.5 collective-permute-start.4
  6.2 0.1 collective-permute-start.6
  6.3 0.7 reshape.90.map_ref
  7.0 1.1 %copy-done.2 = bf16[8,6,6,1024]{3,0,2,1:T(8,128)(2,1)S(1)} copy-done((bf16[8,6,6,1024]{3,0,2,1:T(8,128)(2,1)S(1)}, bf16[8,6,6,1024]{3,0,2,1:T(8,128)(2,1)}, u32[]{:S(2)}) %copy-start.2) | copy-done | bytes 589848
  8.1 1.0 %shard_map.91 = bf16[8,16,1024]{2,1,0:T(8,128)(2,1)} custom-call(s32[1]{0:T(128)} %bitcast.7.me_ref, s32[8,8]{1,0:T(8,128)S(1)} %reshape.90.map_ref, bf16[6,6,8,1024]{3,2,1,0:T(8,128)(2,1)S(1)} %bitcast.17), custom_call_target="tpu_custom_call" | custom-call | tf_op jit(solution)/shard_map/pallas_call | solution.py:79
  9.1 5.3 %all-to-all-start = ((bf16[8,16,1024]{2,1,0:T(8,128)(2,1)}), bf16[8,16,1024]{2,1,0:T(8,128)(2,1)S(1)}, u32[]{:S(2)}, u32[]{:S(2)}) async-start(bf16[8,16,1024]{2,1,0:T(8,128)(2,1)} %shard_map.91), calls=%async_computation | async-start | bytes 524288 | tf_op jit(solution)/shard_map/all_to_all | solution.py:388
  14.4 0.7 reshape.92
  15.2 0.1 select_reduce_fusion.1
  15.3 0.8 reshape.91
  16.0 0.1 select_reduce_fusion
  16.2 0.1 lt.59
  16.3 0.1 lt.60
  16.4 0.1 lt.66
  16.4 0.1 lt.67
  16.5 0.1 reduce_or.36
  16.6 0.1 and.46
  16.7 0.1 and.47
  16.8 0.1 add.63
  16.9 0.1 add.64
  17.0 0.1 lt.57
  17.1 0.1 lt.64
  17.1 0.1 add.68
  17.3 0.2 fusion.1
  17.4 0.1 fusion.3
  17.5 0.1 fusion.4
  17.6 0.7 reshape.97
  18.3 1.6 %collective-permute-start.7 = (bf16[192,1024]{1,0:T(8,128)(2,1)S(1)}, bf16[192,1024]{1,0:T(8,128)(2,1)S(1)}, u32[]{:S(2)}, u32[]{:S(2)}) collective-permute-start(bf16[192,1024]{1,0:T(8,128)(2,1)S(1)} %collective-permute-done.5.refs_2_), channel_id=1, source_target_pairs={{0,1},{1,0},{2,3},{3,2},{4,5},{5,4},{6,7},{7,6},{8,9},{9,8},{10,11... | collective-permute-start | bytes 1179656 | tf_op jit(solution)/shard_map/ppermute | solution.py:23
  19.9 4.8 %collective-permute-done.4.refs_1_ = bf16[192,1024]{1,0:T(8,128)(2,1)S(1)} collective-permute-done((bf16[192,1024]{1,0:T(8,128)(2,1)S(1)}, bf16[192,1024]{1,0:T(8,128)(2,1)S(1)}, u32[]{:S(2)}, u32[]{:S(2)}) %collective-permute-start.4) | collective-permute-done | bytes 393248 | tf_op jit(solution)/shard_map/ppermute | solution.py:23
  24.7 0.1 shard_map.92.refs_0_
  24.7 1.6 %collective-permute-start = (bf16[80,1024]{1,0:T(8,128)(2,1)S(1)}, bf16[80,1024]{1,0:T(8,128)(2,1)S(1)}, u32[]{:S(2)}, u32[]{:S(2)}) collective-permute-start(bf16[80,1024]{1,0:T(8,128)(2,1)S(1)} %shard_map.92.refs_0_), channel_id=1, source_target_pairs={{0,1},{1,0},{2,3},{3,2},{4,5},{5,4},{6,7},{7,6},{8,9},{9,8},{10,11... | collective-permute-start | bytes 491528 | tf_op jit(solution)/shard_map/ppermute | solution.py:23
  26.3 2.0 %collective-permute-start.1 = (bf16[80,1024]{1,0:T(8,128)(2,1)S(1)}, bf16[80,1024]{1,0:T(8,128)(2,1)S(1)}, u32[]{:S(2)}, u32[]{:S(2)}) collective-permute-start(bf16[80,1024]{1,0:T(8,128)(2,1)S(1)} %shard_map.92.refs_0_), channel_id=1, source_target_pairs={{0,2},{1,3},{2,0},{3,1},{4,6},{5,7},{6,4},{7,5},{8,10},{9,11},{10,... | collective-permute-start | bytes 491528 | tf_op jit(solution)/shard_map/ppermute | solution.py:23
  28.4 0.1 pad_add_fusion.1.idx_ref
  28.4 0.7 reshape.99
  29.1 4.6 %copy-done = bf16[4096,3,512]{2,0,1:T(8,128)(2,1)S(1)} copy-done((bf16[4096,3,512]{2,0,1:T(8,128)(2,1)S(1)}, bf16[4096,3,512]{2,0,1:T(8,128)(2,1)}, u32[]{:S(2)}) %copy-start) | copy-done | bytes 12582936
  33.7 2.2 %copy-done.1 = bf16[512,4096]{1,0:T(8,128)(2,1)S(1)} copy-done((bf16[512,4096]{1,0:T(8,128)(2,1)S(1)}, bf16[512,4096]{1,0:T(8,128)(2,1)}, u32[]{:S(2)}) %copy-start.1) | copy-done | bytes 4194328
  35.9 1.1 %shard_map.93 = (bf16[3,4096,512]{2,1,0:T(8,128)(2,1)S(1)}, bf16[512,4096]{1,0:T(8,128)(2,1)S(1)}) custom-call(bf16[3,4096,512]{2,1,0:T(8,128)(2,1)S(1)} %bitcast.16, bf16[512,4096]{1,0:T(8,128)(2,1)S(1)} %copy-done.1), custom_call_target="tpu_custom_call" | custom-call | tf_op jit(solution)/shard_map/pallas_call | solution.py:124
  37.0 1.4 %shard_map.95 = (f32[3,384,512]{2,1,0:T(8,128)S(1)}, f32[384,128]{1,0:T(8,128)S(1)}) custom-call(s32[1]{0:T(128)} %bitcast.2.idx_ref, bf16[192,1024]{1,0:T(8,128)(2,1)S(1)} %get-tuple-element.64.refs_0_, bf16[192,1024]{1,0:T(8,128)(2,1)S(1)} %get-tuple-element.63.refs_1_, f32[4,1,1024]{2,1,0:T(1,128)S(1)} %bitcast.18, ...), custom_call_target="tpu_custom_call" | custom-call | tf_op jit(solution)/shard_map/pallas_call | solution.py:182
  38.5 0.1 pad_add_fusion.idx_ref
  38.6 1.3 %collective-permute-done.1.refs_2_ = bf16[80,1024]{1,0:T(8,128)(2,1)S(1)} collective-permute-done((bf16[80,1024]{1,0:T(8,128)(2,1)S(1)}, bf16[80,1024]{1,0:T(8,128)(2,1)S(1)}, u32[]{:S(2)}, u32[]{:S(2)}) %collective-permute-start.1) | collective-permute-done | bytes 163872 | tf_op jit(solution)/shard_map/ppermute | solution.py:23
  39.9 0.7 copy-done.3
  40.6 0.9 %copy-done.4 = bf16[80,1024]{1,0:T(8,128)(2,1)S(1)} copy-done((bf16[80,1024]{1,0:T(8,128)(2,1)S(1)}, bf16[80,1024]{1,0:T(8,128)(2,1)}, u32[]{:S(2)}) %copy-start.4) | copy-done | bytes 163864
  41.5 3.5 %shard_map.94 = (bf16[3,80,512]{2,1,0:T(8,128)(2,1)S(1)}, bf16[80,1024]{1,0:T(8,128)(2,1)S(1)}) custom-call(s32[4]{0:T(128)S(1)} %pad_add_fusion.idx_ref, bf16[80,1024]{1,0:T(8,128)(2,1)S(1)} %shard_map.92.refs_0_, bf16[80,1024]{1,0:T(8,128)(2,1)S(1)} %collective-permute-done.refs_1_, bf16[80,1024]{1,0:T(8,128)(2,1)S(1)} %copy-done.4, ...), custom_call_target="tpu_custom_call" | custom-call | tf_op jit(solution)/shard_map/pallas_call | solution.py:226
  45.0 3.3 %shard_map.96 = (f32[3,384,512]{2,1,0:T(8,128)S(1)}, f32[384,128]{1,0:T(8,128)S(1)}) custom-call(s32[2]{0:T(128)S(1)} %pad_add_fusion.1.idx_ref, bf16[192,1024]{1,0:T(8,128)(2,1)S(1)} %collective-permute-done.3.refs_0_, bf16[192,1024]{1,0:T(8,128)(2,1)S(1)} %collective-permute-done.4.refs_1_, bf16[192,1024]{1,0:T(8,128)(2,1)S(1)} %collective-permute-done.5.refs_2_, ...), custom_call_target="tpu_custom_call" | custom-call | tf_op jit(solution)/shard_map/pallas_call | solution.py:182
  48.3 0.1 broadcast_in_dim.45.text_row_ref
  48.4 4.2 %shard_map.97 = (bf16[384,512]{1,0:T(8,128)(2,1)S(1)}, bf16[192,1024]{1,0:T(8,128)(2,1)S(1)}, bf16[192,1024]{1,0:T(8,128)(2,1)S(1)}) custom-call(s32[1]{0:T(128)} %bitcast.5.idx_ref, bf16[192,1024]{1,0:T(8,128)(2,1)S(1)} %collective-permute-done.7.top_ref, bf16[192,1024]{1,0:T(8,128)(2,1)} %collective-permute-done.8.bottom_ref, f32[4,1,1024]{2,1,0:T(1,128)S(1)} %bitcast.21, ...), custom_call_target="tpu_custom_call" | custom-call | tf_op jit(solution)/shard_map/pallas_call | solution.py:295
  52.6 0.7 collective-permute-start.13
  53.4 1.4 %collective-permute-start.9 = (bf16[192,1024]{1,0:T(8,128)(2,1)S(1)}, bf16[192,1024]{1,0:T(8,128)(2,1)S(1)}, u32[]{:S(2)}, u32[]{:S(2)}) collective-permute-start(bf16[192,1024]{1,0:T(8,128)(2,1)S(1)} %get-tuple-element.55), channel_id=1, source_target_pairs={{0,1},{1,0},{2,3},{3,2},{4,5},{5,4},{6,7},{7,6},{8,9},{9,8},{10,11... | collective-permute-start | bytes 1179656 | tf_op jit(solution)/shard_map/ppermute | solution.py:23
  54.8 0.6 shard_map.100
  55.4 0.6 shard_map.99
  56.0 0.7 collective-permute-start.11
  56.7 1.4 %collective-permute-start.12 = (bf16[192,1024]{1,0:T(8,128)(2,1)S(1)}, bf16[192,1024]{1,0:T(8,128)(2,1)S(1)}, u32[]{:S(2)}, u32[]{:S(2)}) collective-permute-start(bf16[192,1024]{1,0:T(8,128)(2,1)S(1)} %get-tuple-element.58), channel_id=1, source_target_pairs={{0,2},{1,3},{2,0},{3,1},{4,6},{5,7},{6,4},{7,5},{8,10},{9,11},{10,... | collective-permute-start | bytes 1179656 | tf_op jit(solution)/shard_map/ppermute | solution.py:23
  58.0 6.7 %collective-permute-done.13 = bf16[192,1024]{1,0:T(8,128)(2,1)S(1)} collective-permute-done((bf16[192,1024]{1,0:T(8,128)(2,1)S(1)}, bf16[192,1024]{1,0:T(8,128)(2,1)S(1)}, u32[]{:S(2)}, u32[]{:S(2)}) %collective-permute-start.13) | collective-permute-done | bytes 393248 | tf_op jit(solution)/shard_map/ppermute | solution.py:23
  64.8 0.1 add_convert_fusion
  64.9 1.6 %collective-permute-start.14 = (bf16[192,1024]{1,0:T(8,128)(2,1)S(1)}, bf16[192,1024]{1,0:T(8,128)(2,1)S(1)}, u32[]{:S(2)}, u32[]{:S(2)}) collective-permute-start(bf16[192,1024]{1,0:T(8,128)(2,1)S(1)} %add_convert_fusion), channel_id=1, source_target_pairs={{0,1},{1,0},{2,3},{3,2},{4,5},{5,4},{6,7},{7,6},{8,9},{9,8},{10,11... | collective-permute-start | bytes 1179656 | tf_op jit(solution)/shard_map/ppermute | solution.py:23
  66.5 0.1 add_convert_fusion.1
  66.6 0.7 collective-permute-start.10
  67.3 0.4 fusion.base_ref
  67.6 0.6 shard_map.98
  68.3 5.6 %collective-permute-done.11.refs_2_ = bf16[192,1024]{1,0:T(8,128)(2,1)S(1)} collective-permute-done((bf16[192,1024]{1,0:T(8,128)(2,1)S(1)}, bf16[192,1024]{1,0:T(8,128)(2,1)S(1)}, u32[]{:S(2)}, u32[]{:S(2)}) %collective-permute-start.11) | collective-permute-done | bytes 393248 | tf_op jit(solution)/shard_map/ppermute | solution.py:23
  73.9 4.7 %collective-permute-done.14.refs_5_ = bf16[192,1024]{1,0:T(8,128)(2,1)S(1)} collective-permute-done((bf16[192,1024]{1,0:T(8,128)(2,1)S(1)}, bf16[192,1024]{1,0:T(8,128)(2,1)S(1)}, u32[]{:S(2)}, u32[]{:S(2)}) %collective-permute-start.14) | collective-permute-done | bytes 393248 | tf_op jit(solution)/shard_map/ppermute | solution.py:23
  78.6 1.2 %shard_map.101 = bf16[384,1024]{1,0:T(8,128)(2,1)} custom-call(bf16[384,1024]{1,0:T(8,128)(2,1)S(1)} %fusion.base_ref, f32[192,1024]{1,0:T(8,128)S(1)} %get-tuple-element.53.refs_0_, bf16[192,1024]{1,0:T(8,128)(2,1)S(1)} %collective-permute-done.10.refs_1_, bf16[192,1024]{1,0:T(8,128)(2,1)S(1)} %collective-permute-done.11.refs_2_, ...), custom_call_target="tpu_custom_call" | custom-call | bytes 3932160 | tf_op jit(solution)/shard_map/pallas_call | solution.py:347
  (31 shorter events, 0.2 us)
Async XLA Ops:
  1.2 17.1 %collective-permute-start.5 = (bf16[192,1024]{1,0:T(8,128)(2,1)S(1)}, bf16[192,1024]{1,0:T(8,128)(2,1)S(1)}, u32[]{:S(2)}, u32[]{:S(2)}) collective-permute-start(bf16[192,1024]{1,0:T(8,128)(2,1)S(1)} %get-tuple-element.64.refs_0_), channel_id=1, source_target_pairs={{0,2},{1,3},{2,0},{3,1},{4,6},{5,7},{6,4},{7,5},{8,10},{9,11},{10,... | collective-permute-start | bytes 1179656 | tf_op jit(solution)/shard_map/ppermute | solution.py:23
  4.2 22.1 %collective-permute-start.3 = (bf16[192,1024]{1,0:T(8,128)(2,1)S(1)}, bf16[192,1024]{1,0:T(8,128)(2,1)S(1)}, u32[]{:S(2)}, u32[]{:S(2)}) collective-permute-start(bf16[192,1024]{1,0:T(8,128)(2,1)S(1)} %get-tuple-element.64.refs_0_), channel_id=1, source_target_pairs={{0,1},{1,0},{2,3},{3,2},{4,5},{5,4},{6,7},{7,6},{8,9},{9,8},{10,11... | collective-permute-start | bytes 1179656 | tf_op jit(solution)/shard_map/ppermute | solution.py:23
  5.7 19.0 %collective-permute-start.4 = (bf16[192,1024]{1,0:T(8,128)(2,1)S(1)}, bf16[192,1024]{1,0:T(8,128)(2,1)S(1)}, u32[]{:S(2)}, u32[]{:S(2)}) collective-permute-start(bf16[192,1024]{1,0:T(8,128)(2,1)S(1)} %get-tuple-element.63.refs_1_), channel_id=1, source_target_pairs={{0,1},{1,0},{2,3},{3,2},{4,5},{5,4},{6,7},{7,6},{8,9},{9,8},{10,11... | collective-permute-start | bytes 1179656 | tf_op jit(solution)/shard_map/ppermute | solution.py:23
  6.2 22.1 %collective-permute-start.6 = (bf16[192,1024]{1,0:T(8,128)(2,1)S(1)}, bf16[192,1024]{1,0:T(8,128)(2,1)S(1)}, u32[]{:S(2)}, u32[]{:S(2)}) collective-permute-start(bf16[192,1024]{1,0:T(8,128)(2,1)S(1)} %get-tuple-element.63.refs_1_), channel_id=1, source_target_pairs={{0,2},{1,3},{2,0},{3,1},{4,6},{5,7},{6,4},{7,5},{8,10},{9,11},{10,... | collective-permute-start | bytes 1179656 | tf_op jit(solution)/shard_map/ppermute | solution.py:23
  7.0 1.1 %copy-start.2 = (bf16[8,6,6,1024]{3,0,2,1:T(8,128)(2,1)S(1)}, bf16[8,6,6,1024]{3,0,2,1:T(8,128)(2,1)}, u32[]{:S(2)}) copy-start(bf16[8,6,6,1024]{3,0,2,1:T(8,128)(2,1)} %param.10) | copy-start | bytes 1769476
  9.1 15.6 %all-to-all-start = ((bf16[8,16,1024]{2,1,0:T(8,128)(2,1)}), bf16[8,16,1024]{2,1,0:T(8,128)(2,1)S(1)}, u32[]{:S(2)}, u32[]{:S(2)}) async-start(bf16[8,16,1024]{2,1,0:T(8,128)(2,1)} %shard_map.91), calls=%async_computation | async-start | bytes 524288 | tf_op jit(solution)/shard_map/all_to_all | solution.py:388
  18.3 30.0 %collective-permute-start.7 = (bf16[192,1024]{1,0:T(8,128)(2,1)S(1)}, bf16[192,1024]{1,0:T(8,128)(2,1)S(1)}, u32[]{:S(2)}, u32[]{:S(2)}) collective-permute-start(bf16[192,1024]{1,0:T(8,128)(2,1)S(1)} %collective-permute-done.5.refs_2_), channel_id=1, source_target_pairs={{0,1},{1,0},{2,3},{3,2},{4,5},{5,4},{6,7},{7,6},{8,9},{9,8},{10,11... | collective-permute-start | bytes 1179656 | tf_op jit(solution)/shard_map/ppermute | solution.py:23
  24.7 23.6 %collective-permute-start.8 = (bf16[192,1024]{1,0:T(8,128)(2,1)S(1)}, bf16[192,1024]{1,0:T(8,128)(2,1)}, u32[]{:S(2)}, u32[]{:S(2)}) collective-permute-start(bf16[192,1024]{1,0:T(8,128)(2,1)S(1)} %collective-permute-done.4.refs_1_), channel_id=1, source_target_pairs={{0,2},{1,3},{2,0},{3,1},{4,6},{5,7},{6,4},{7,5},{8,10},{9,11},{10,... | collective-permute-start | bytes 1179656 | tf_op jit(solution)/shard_map/ppermute | solution.py:23
  24.7 13.8 %collective-permute-start = (bf16[80,1024]{1,0:T(8,128)(2,1)S(1)}, bf16[80,1024]{1,0:T(8,128)(2,1)S(1)}, u32[]{:S(2)}, u32[]{:S(2)}) collective-permute-start(bf16[80,1024]{1,0:T(8,128)(2,1)S(1)} %shard_map.92.refs_0_), channel_id=1, source_target_pairs={{0,1},{1,0},{2,3},{3,2},{4,5},{5,4},{6,7},{7,6},{8,9},{9,8},{10,11... | collective-permute-start | bytes 491528 | tf_op jit(solution)/shard_map/ppermute | solution.py:23
  26.3 13.6 %collective-permute-start.1 = (bf16[80,1024]{1,0:T(8,128)(2,1)S(1)}, bf16[80,1024]{1,0:T(8,128)(2,1)S(1)}, u32[]{:S(2)}, u32[]{:S(2)}) collective-permute-start(bf16[80,1024]{1,0:T(8,128)(2,1)S(1)} %shard_map.92.refs_0_), channel_id=1, source_target_pairs={{0,2},{1,3},{2,0},{3,1},{4,6},{5,7},{6,4},{7,5},{8,10},{9,11},{10,... | collective-permute-start | bytes 491528 | tf_op jit(solution)/shard_map/ppermute | solution.py:23
  28.3 12.2 %collective-permute-start.2 = (bf16[80,1024]{1,0:T(8,128)(2,1)S(1)}, bf16[80,1024]{1,0:T(8,128)(2,1)}, u32[]{:S(2)}, u32[]{:S(2)}) collective-permute-start(bf16[80,1024]{1,0:T(8,128)(2,1)S(1)} %shard_map.92.refs_0_), channel_id=1, source_target_pairs={{0,3},{1,2},{2,1},{3,0},{4,7},{5,6},{6,5},{7,4},{8,11},{9,10},{10,... | collective-permute-start | bytes 491528 | tf_op jit(solution)/shard_map/ppermute | solution.py:23
  29.1 4.6 %copy-start = (bf16[4096,3,512]{2,0,1:T(8,128)(2,1)S(1)}, bf16[4096,3,512]{2,0,1:T(8,128)(2,1)}, u32[]{:S(2)}) copy-start(bf16[4096,3,512]{2,0,1:T(8,128)(2,1)} %param.16) | copy-start | bytes 37748740
  33.7 2.2 %copy-start.1 = (bf16[512,4096]{1,0:T(8,128)(2,1)S(1)}, bf16[512,4096]{1,0:T(8,128)(2,1)}, u32[]{:S(2)}) copy-start(bf16[512,4096]{1,0:T(8,128)(2,1)} %out_ref) | copy-start | bytes 12582916
  39.9 0.7 copy-start.3
  40.6 0.9 %copy-start.4 = (bf16[80,1024]{1,0:T(8,128)(2,1)S(1)}, bf16[80,1024]{1,0:T(8,128)(2,1)}, u32[]{:S(2)}) copy-start(bf16[80,1024]{1,0:T(8,128)(2,1)} %copy-done.3) | copy-start | bytes 491524
  52.6 12.1 %collective-permute-start.13 = (bf16[192,1024]{1,0:T(8,128)(2,1)S(1)}, bf16[192,1024]{1,0:T(8,128)(2,1)S(1)}, u32[]{:S(2)}, u32[]{:S(2)}) collective-permute-start(bf16[192,1024]{1,0:T(8,128)(2,1)S(1)} %get-tuple-element.60), channel_id=1, source_target_pairs={{0,2},{1,3},{2,0},{3,1},{4,6},{5,7},{6,4},{7,5},{8,10},{9,11},{10,... | collective-permute-start | bytes 1179656 | tf_op jit(solution)/shard_map/ppermute | solution.py:23
  53.4 13.1 %collective-permute-start.9 = (bf16[192,1024]{1,0:T(8,128)(2,1)S(1)}, bf16[192,1024]{1,0:T(8,128)(2,1)S(1)}, u32[]{:S(2)}, u32[]{:S(2)}) collective-permute-start(bf16[192,1024]{1,0:T(8,128)(2,1)S(1)} %get-tuple-element.55), channel_id=1, source_target_pairs={{0,1},{1,0},{2,3},{3,2},{4,5},{5,4},{6,7},{7,6},{8,9},{9,8},{10,11... | collective-permute-start | bytes 1179656 | tf_op jit(solution)/shard_map/ppermute | solution.py:23
  55.4 11.9 %copy-start.5 = (bf16[384,1024]{1,0:T(8,128)(2,1)S(1)}, bf16[384,1024]{1,0:T(8,128)(2,1)}, u32[]{:S(2)}) copy-start(bf16[384,1024]{1,0:T(8,128)(2,1)} %param.9) | copy-start | bytes 2359300
  56.0 17.8 %collective-permute-start.11 = (bf16[192,1024]{1,0:T(8,128)(2,1)S(1)}, bf16[192,1024]{1,0:T(8,128)(2,1)S(1)}, u32[]{:S(2)}, u32[]{:S(2)}) collective-permute-start(bf16[192,1024]{1,0:T(8,128)(2,1)S(1)} %get-tuple-element.56), channel_id=1, source_target_pairs={{0,1},{1,0},{2,3},{3,2},{4,5},{5,4},{6,7},{7,6},{8,9},{9,8},{10,11... | collective-permute-start | bytes 1179656 | tf_op jit(solution)/shard_map/ppermute | solution.py:23
  56.7 17.2 %collective-permute-start.12 = (bf16[192,1024]{1,0:T(8,128)(2,1)S(1)}, bf16[192,1024]{1,0:T(8,128)(2,1)S(1)}, u32[]{:S(2)}, u32[]{:S(2)}) collective-permute-start(bf16[192,1024]{1,0:T(8,128)(2,1)S(1)} %get-tuple-element.58), channel_id=1, source_target_pairs={{0,2},{1,3},{2,0},{3,1},{4,6},{5,7},{6,4},{7,5},{8,10},{9,11},{10,... | collective-permute-start | bytes 1179656 | tf_op jit(solution)/shard_map/ppermute | solution.py:23
  64.9 13.7 %collective-permute-start.14 = (bf16[192,1024]{1,0:T(8,128)(2,1)S(1)}, bf16[192,1024]{1,0:T(8,128)(2,1)S(1)}, u32[]{:S(2)}, u32[]{:S(2)}) collective-permute-start(bf16[192,1024]{1,0:T(8,128)(2,1)S(1)} %add_convert_fusion), channel_id=1, source_target_pairs={{0,1},{1,0},{2,3},{3,2},{4,5},{5,4},{6,7},{7,6},{8,9},{9,8},{10,11... | collective-permute-start | bytes 1179656 | tf_op jit(solution)/shard_map/ppermute | solution.py:23
  66.6 12.0 %collective-permute-start.10 = (bf16[192,1024]{1,0:T(8,128)(2,1)S(1)}, bf16[192,1024]{1,0:T(8,128)(2,1)S(1)}, u32[]{:S(2)}, u32[]{:S(2)}) collective-permute-start(bf16[192,1024]{1,0:T(8,128)(2,1)S(1)} %add_convert_fusion.1), channel_id=1, source_target_pairs={{0,2},{1,3},{2,0},{3,1},{4,6},{5,7},{6,4},{7,5},{8,10},{9,11},{10,... | collective-permute-start | bytes 1179656 | tf_op jit(solution)/shard_map/ppermute | solution.py:23

commit v3 on v2

v3 whole, which is shorter than its diff:
```python
import functools

import jax
import jax.numpy as jnp
from jax import lax
from jax.experimental import pallas as pl
from jax.experimental.pallas import tpu as pltpu
from jax.sharding import PartitionSpec as P

D = 4096
HD = 128
EPS = 1e-05
LOG2E = 1.4426950408889634
TINY = pl.CostEstimate(flops=0, bytes_accessed=0, transcendentals=0)


def round_up(n, m):
    return -(-n // m) * m


def swap(x, s, axis="tensor"):
    n = lax.axis_size(axis)
    return lax.ppermute(x, axis, [(i, i ^ s) for i in range(n)])


def in_hbm(x):
    return pltpu.with_memory_space_constraint(x, pltpu.HBM)


def low_bit(s):
    return s & -s


def high_bit(s):
    return 1 << (s.bit_length() - 1)


def by_bits(n, reverse=False):
    return sorted(range(1, n), key=lambda s: (bin(s).count("1"), s), reverse=reverse)


def gather_halves(top, bottom, n):
    blocks = {0: (top, bottom)}
    for s in by_bits(n):
        low, high = low_bit(s), high_bit(s)
        if low == high:
            other = (swap(top, s), swap(bottom, s))
        else:
            other = (swap(blocks[s ^ low][0], low), swap(blocks[s ^ high][1], high))
        blocks[s] = other
    return blocks


def vmem_specs(n):
    return [pl.BlockSpec(memory_space=pltpu.VMEM)] * n


def params(mib):
    return pltpu.CompilerParams(vmem_limit_bytes=mib * 1024 * 1024)


def split_kernel(x_ref, top_ref, bottom_ref, sem_ref):
    half = top_ref.shape[0]
    copies = [
        pltpu.make_async_copy(x_ref.at[pl.ds(side * half, half)], out_ref, sem_ref.at[side])
        for side, out_ref in enumerate((top_ref, bottom_ref))
    ]
    for copy in copies:
        copy.start()
    for copy in copies:
        copy.wait()


def split_rows(x):
    half = pltpu.VMEM((x.shape[0] // 2, x.shape[1]), x.dtype)
    return pl.pallas_call(
        split_kernel,
        out_shape=(half, half),
        in_specs=[pl.BlockSpec(memory_space=pltpu.HBM)],
        out_specs=tuple(vmem_specs(2)),
        scratch_shapes=[pltpu.SemaphoreType.DMA((2,))],
        compiler_params=params(4),
        cost_estimate=TINY,
    )(in_hbm(x))


def pool_kernel(me_ref, req_ref, x_ref, *refs):
    outs, tmp_ref = refs[:-1], refs[-1]
    n_req = len(outs)
    side, img_dev = x_ref.shape[0], x_ref.shape[2]
    half = side // 2
    me = me_ref[0]
    rows = lax.broadcasted_iota(jnp.int32, (n_req, img_dev), 0)
    cols = lax.broadcasted_iota(jnp.int32, (n_req, img_dev), 1)
    away = jnp.full((n_req, img_dev), -1, jnp.int32)
    for k in range(img_dev):
        away = jnp.where(cols == k, req_ref[me * img_dev + k] ^ me, away)
    onehot = (rows == away).astype(jnp.bfloat16)
    tmp_ref[...] = jnp.zeros_like(tmp_ref)
    for i in range(half):
        for j in range(half):
            total = x_ref[2 * i, 2 * j].astype(jnp.float32)
            for a, b in ((0, 1), (1, 0), (1, 1)):
                total += x_ref[2 * i + a, 2 * j + b].astype(jnp.float32)
            pooled = (total * 0.25).astype(jnp.bfloat16)
            tmp_ref[:, i * half + j, :] = jnp.dot(onehot, pooled, preferred_element_type=jnp.float32)
    for s in range(n_req):
        outs[s][...] = tmp_ref[s].astype(jnp.bfloat16)


def pool_images(me, image_request, patches, n_req):
    side, _, img_dev, width = patches.shape
    padded = round_up((side // 2) ** 2, 16)
    return pl.pallas_call(
        pool_kernel,
        out_shape=(jax.ShapeDtypeStruct((padded, width), jnp.bfloat16),) * n_req,
        in_specs=[pl.BlockSpec(memory_space=pltpu.SMEM)] * 2 + vmem_specs(1),
        out_specs=tuple(vmem_specs(n_req)),
        scratch_shapes=[pltpu.VMEM((n_req, padded, width), jnp.float32)],
        compiler_params=params(24),
        cost_estimate=TINY,
    )(me, image_request, patches)


def pack_kernel(region, gain_ref, *refs):
    recs, (out_ref, tmp_ref) = refs[:-2], refs[-2:]
    for r, rec_ref in enumerate(recs):
        tmp_ref[region * r : region * (r + 1)] = rec_ref[...].astype(jnp.float32)[:region]
    done = region * len(recs)
    rest = tmp_ref.shape[0] - done
    tmp_ref[done:] = jnp.broadcast_to(gain_ref[0:1, :], (rest, gain_ref.shape[1]))
    out_ref[...] = tmp_ref[...].astype(jnp.bfloat16)


def pack_images(received, gain, region, n_img):
    width = gain.shape[1]
    return pl.pallas_call(
        functools.partial(pack_kernel, region),
        out_shape=jax.ShapeDtypeStruct((n_img, width), jnp.bfloat16),
        in_specs=vmem_specs(1 + len(received)),
        out_specs=pl.BlockSpec(memory_space=pltpu.VMEM),
        scratch_shapes=[pltpu.VMEM((n_img, width), jnp.float32)],
        compiler_params=params(24),
        cost_estimate=TINY,
    )(gain, *received)


def place_kernel(n_req, half, me_ref, req_ref, start_ref, high_ref, wide_ref, place_ref, text_row_ref, key_ref):
    rows, n_img = place_ref.shape
    img_dev = req_ref.shape[0] // n_req
    me = me_ref[0]
    lane = lax.broadcasted_iota(jnp.int32, (1, n_img), 1)

    def one_source(s, carry):
        pos, spot = carry
        source = me ^ s

        def one_image(k, found):
            i = source * img_dev + k
            hit = req_ref[i] == me
            values = (start_ref[i], high_ref[i] // 2, wide_ref[i] // 2)
            return tuple(jnp.where(hit, new, old) for new, old in zip(values, found))

        none = jnp.int32(-1)
        start, high, wide = lax.fori_loop(0, img_dev, one_image, (none, none, none), unroll=img_dev <= 8)
        for i in range(half):
            for j in range(half):
                cell = i * half + j
                here = lane == s * half * half + cell
                has = start >= 0
                valid = has & (i < high) & (j < wide)
                pos = jnp.where(here, jnp.where(valid, start + i * wide + j, none), pos)
                spot = jnp.where(here, jnp.where(has, start + cell, none), spot)
        return pos, spot

    empty = jnp.full((1, n_img), -1, jnp.int32)
    pos, spot = lax.fori_loop(0, n_req, one_source, (empty, empty))
    row = lax.broadcasted_iota(jnp.int32, (rows, n_img), 0)
    placed = (row == pos).astype(jnp.float32)
    region = (row == spot).astype(jnp.float32)
    place = placed.astype(jnp.bfloat16)
    place_ref[...] = place
    text_row_ref[...] = jnp.broadcast_to(1.0 - jnp.sum(placed, axis=1, keepdims=True), text_row_ref.shape)
    ones = jnp.ones((8, n_img), jnp.bfloat16)
    open_keys = (placed - region).astype(jnp.bfloat16)
    count = lax.dot_general(ones, open_keys, (((1,), (1,)), ((), ())), preferred_element_type=jnp.float32)
    key_ref[...] = 1.0 + count


def placement(me, image_request, slot_start, grids, n_req, half, rows, n_img):
    return pl.pallas_call(
        functools.partial(place_kernel, n_req, half),
        out_shape=(
            jax.ShapeDtypeStruct((rows, n_img), jnp.bfloat16),
            jax.ShapeDtypeStruct((rows, 128), jnp.float32),
            jax.ShapeDtypeStruct((8, rows), jnp.float32),
        ),
        in_specs=[pl.BlockSpec(memory_space=pltpu.SMEM)] * 5,
        out_specs=tuple(vmem_specs(3)),
        compiler_params=params(8),
        cost_estimate=TINY,
    )(me, image_request, slot_start, grids[:, 0], grids[:, 1])


def cols_of(ref, owner, width):
    return ref[:, pl.ds(pl.multiple_of(owner * width, width), width)]


def rows_of(ref, j, owner, width):
    return ref[j, pl.ds(pl.multiple_of(owner * width, width), width)]


def scale_rows(x_ref, gain):
    xf = x_ref[...].astype(jnp.float32)
    return (xf * gain).astype(jnp.bfloat16), jnp.sum(xf * xf, axis=1, keepdims=True)


def own_kernel(owners, me_ref, top_ref, bottom_ref, gain_ref, w_ref, acc_ref, ss_ref, held_ref, sem_ref):
    half, width = top_ref.shape
    me = me_ref[0]
    copies = []
    for s in range(owners):
        rows = pl.ds(pl.multiple_of((me ^ s) * width, width), width)
        for j in range(3):
            copies.append(pltpu.make_async_copy(w_ref.at[j, rows], held_ref.at[j, rows], sem_ref.at[s, j]))
    for copy in copies:
        copy.start()
    scaled = []
    for side, x_ref in enumerate((top_ref, bottom_ref)):
        x, total = scale_rows(x_ref, gain_ref[me])
        scaled.append(x)
        ss_ref[pl.ds(side * half, half)] = jnp.broadcast_to(total, (half, 128))
    for j in range(3):
        copies[j].wait()
        weight = rows_of(held_ref, j, me, width)
        for side in range(2):
            acc_ref[j, pl.ds(side * half, half)] = jnp.dot(scaled[side], weight, preferred_element_type=jnp.float32)
    for copy in copies[3:]:
        copy.wait()


def own_part(me, block, gain, w, n_ten):
    half, width = block[0].shape
    rows, cols = 2 * half, w.shape[2]
    return pl.pallas_call(
        functools.partial(own_kernel, n_ten),
        out_shape=(
            jax.ShapeDtypeStruct((3, rows, cols), jnp.float32),
            jax.ShapeDtypeStruct((rows, 128), jnp.float32),
            pltpu.VMEM(w.shape, w.dtype),
        ),
        in_specs=[pl.BlockSpec(memory_space=pltpu.SMEM)] + vmem_specs(3) + [pl.BlockSpec(memory_space=pltpu.HBM)],
        out_specs=tuple(vmem_specs(3)),
        scratch_shapes=[pltpu.SemaphoreType.DMA((n_ten, 3))],
        compiler_params=params(12),
        cost_estimate=TINY,
    )(me, *block, gain, in_hbm(w))


def near_kernel(near, me_ref, *refs):
    n_blk = len(near)
    x_refs, refs = refs[: 2 * n_blk], refs[2 * n_blk :]
    gain_ref, w_ref, acc_in, ss_in, w_out_ref, acc_ref, ss_ref, held_ref, sem_ref = refs
    half, width = x_refs[0].shape
    me = me_ref[0]
    copy = pltpu.make_async_copy(w_out_ref, held_ref, sem_ref)
    copy.start()
    scaled = {}
    for side in range(2):
        rows = pl.ds(side * half, half)
        total = ss_in[rows]
        for b, s in enumerate(near):
            scaled[side, b], part = scale_rows(x_refs[2 * b + side], gain_ref[me ^ s])
            total += part
        ss_ref[rows] = total
    for j in range(3):
        for side in range(2):
            rows = pl.ds(side * half, half)
            acc = acc_in[j, rows]
            for b, s in enumerate(near):
                weight = rows_of(w_ref, j, me ^ s, width)
                acc += jnp.dot(scaled[side, b], weight, preferred_element_type=jnp.float32)
            acc_ref[j, rows] = acc
    copy.wait()


def near_part(near, me, blocks, gain, w, acc, ss, w_out):
    return pl.pallas_call(
        functools.partial(near_kernel, near),
        out_shape=(
            jax.ShapeDtypeStruct(acc.shape, jnp.float32),
            jax.ShapeDtypeStruct(ss.shape, jnp.float32),
            pltpu.VMEM(w_out.shape, w_out.dtype),
        ),
        in_specs=[pl.BlockSpec(memory_space=pltpu.SMEM)]
        + vmem_specs(2 * len(near) + 4)
        + [pl.BlockSpec(memory_space=pltpu.HBM)],
        out_specs=tuple(vmem_specs(3)),
        scratch_shapes=[pltpu.SemaphoreType.DMA],
        compiler_params=params(16),
        cost_estimate=TINY,
    )(me, *[h for b in blocks for h in b], gain, w, acc, ss, in_hbm(w_out))


def image_kernel(n_blk, n_rows, me_ref, *refs):
    x_refs, (gain_ref, w_ref, qkv_ref, own_ref) = refs[:n_blk], refs[n_blk:]
    width = gain_ref.shape[2]
    me = me_ref[0]
    total = 0.0
    for s in range(n_blk):
        xf = x_refs[s][...].astype(jnp.float32)
        total += jnp.sum(xf * xf, axis=1, keepdims=True)
    scale = lax.rsqrt(total / D + EPS)
    total = 0.0
    scaled = []
    for s in range(n_blk):
        xf = x_refs[s][...].astype(jnp.float32)
        merged = (xf * scale * xf[n_rows : n_rows + 1]).astype(jnp.bfloat16)
        if s == 0:
            own_ref[...] = merged
        mf = merged.astype(jnp.float32)
        total += jnp.sum(mf * mf, axis=1, keepdims=True)
        scaled.append((mf * gain_ref[me ^ s]).astype(jnp.bfloat16))
    scale = lax.rsqrt(total / D + EPS)
    for j in range(3):
        acc = 0.0
        for s in range(n_blk):
            weight = rows_of(w_ref, j, me ^ s, width)
            acc += jnp.dot(scaled[s], weight, preferred_element_type=jnp.float32)
        qkv_ref[j] = (acc * scale).astype(jnp.bfloat16)


def image_part(me, blocks, gain, w, n_rows):
    n_blk = len(blocks)
    n_img, width = blocks[0].shape
    cols = w.shape[2]
    return pl.pallas_call(
        functools.partial(image_kernel, n_blk, n_rows),
        out_shape=(
            jax.ShapeDtypeStruct((3, n_img, cols), jnp.bfloat16),
            jax.ShapeDtypeStruct((n_img, width), jnp.bfloat16),
        ),
        in_specs=[pl.BlockSpec(memory_space=pltpu.SMEM)]
        + vmem_specs(n_blk + 2),
        out_specs=tuple(vmem_specs(2)),
        compiler_params=params(16),
        cost_estimate=TINY,
    )(me, *blocks, gain, w)


def final_kernel(far, me_ref, top_ref, bottom_ref, gain_ref, w_ref, acc_ref, ss_ref, img_ref, place_ref, text_row_ref,
                 key_ref, w_out_ref, ctx_ref, far_top_ref, far_bottom_ref, qkv_ref):
    half, width = top_ref.shape
    rows, cols = 2 * half, ctx_ref.shape[1]
    owner = me_ref[0] ^ far
    scaled, scales = [], []
    for side, x_ref in enumerate((top_ref, bottom_ref)):
        part = pl.ds(side * half, half)
        x, total = scale_rows(x_ref, gain_ref[owner])
        scaled.append(x)
        total = ss_ref[part] + total
        scales.append((lax.rsqrt(total / D + EPS) * text_row_ref[part])[:, :1])
    for j in range(3):
        weight = rows_of(w_ref, j, owner, width)
        for side in range(2):
            part = pl.ds(side * half, half)
            prod = jnp.dot(scaled[side], weight, preferred_element_type=jnp.float32)
            put = jnp.dot(place_ref[part], img_ref[j], preferred_element_type=jnp.float32)
            qkv_ref[j, part] = ((prod + acc_ref[j, part]) * scales[side] + put).astype(jnp.bfloat16)
    step = 128
    heads = [pl.ds(h * HD, HD) for h in range(cols // HD)]
    for r in range(rows // step):
        here, last = pl.ds(r * step, step), (r + 1) * step
        row = lax.broadcasted_iota(jnp.int32, (step, last), 0) + r * step
        col = lax.broadcasted_iota(jnp.int32, (step, last), 1)
        bias = jnp.where((row >= col) & (key_ref[0:1, pl.ds(0, last)] > 0.5), 0.0, -1e30)
        scores = [
            lax.dot_general(
                qkv_ref[0, here, lanes],
                qkv_ref[1, pl.ds(0, last), lanes],
                (((1,), (1,)), ((), ())),
                preferred_element_type=jnp.float32,
            )
            for lanes in heads
        ]
        scores = [x * (LOG2E / HD**0.5) + bias for x in scores]
        tops = [jnp.max(x, axis=1, keepdims=True) for x in scores]
        expo = [jnp.exp2(x - top) for x, top in zip(scores, tops)]
        sums = [jnp.sum(x, axis=1, keepdims=True) for x in expo]
        outs = [
            jnp.dot(x.astype(jnp.bfloat16), qkv_ref[2, pl.ds(0, last), lanes], preferred_element_type=jnp.float32)
            for x, lanes in zip(expo, heads)
        ]
        for lanes, out, total in zip(heads, outs, sums):
            ctx_ref[here, lanes] = (out / total).astype(jnp.bfloat16)
    weight = cols_of(w_out_ref, owner, width)
    for side, out_ref in enumerate((far_top_ref, far_bottom_ref)):
        out_ref[...] = jnp.dot(
            ctx_ref[pl.ds(side * half, half)], weight, preferred_element_type=jnp.float32
        ).astype(jnp.bfloat16)


def final_part(far, me, block, gain, w, acc, ss, img, place, text_row, key_ok, w_out):
    half, width = block[0].shape
    rows, cols = 2 * half, w.shape[2]
    return pl.pallas_call(
        functools.partial(final_kernel, far),
        out_shape=(
            jax.ShapeDtypeStruct((rows, cols), jnp.bfloat16),
            jax.ShapeDtypeStruct((half, width), jnp.bfloat16),
            jax.ShapeDtypeStruct((half, width), jnp.bfloat16),
        ),
        in_specs=[pl.BlockSpec(memory_space=pltpu.SMEM)]
        + vmem_specs(11),
        out_specs=tuple(vmem_specs(3)),
        scratch_shapes=[pltpu.VMEM((3, rows, cols), jnp.bfloat16)],
        compiler_params=params(16),
        cost_estimate=TINY,
    )(me, *block, gain, w, acc, ss, img, place, text_row, key_ok, w_out)


def out_kernel(away, me_ref, ctx_ref, w_ref, top_ref, bottom_ref):
    half, width = top_ref.shape
    weight = cols_of(w_ref, me_ref[0] ^ away, width)
    for side, out_ref in enumerate((top_ref, bottom_ref)):
        out_ref[...] = jnp.dot(
            ctx_ref[pl.ds(side * half, half)], weight, preferred_element_type=jnp.float32
        ).astype(out_ref.dtype)


def out_part(away, me, ctx, w, width, dtype=jnp.bfloat16):
    rows, depth = ctx.shape
    return pl.pallas_call(
        functools.partial(out_kernel, away),
        out_shape=(
            jax.ShapeDtypeStruct((rows // 2, width), dtype),
            jax.ShapeDtypeStruct((rows // 2, width), dtype),
        ),
        in_specs=[pl.BlockSpec(memory_space=pltpu.SMEM)] + vmem_specs(2),
        out_specs=tuple(vmem_specs(2)),
        compiler_params=params(16),
        cost_estimate=TINY,
    )(me, ctx, w)


def add_kernel(n_top, base_ref, *refs):
    out_ref, tmp_ref, sem_ref = refs[-3:]
    refs = refs[:-3]
    half = base_ref.shape[0] // 2
    copies = []
    for side, terms in enumerate((refs[:n_top], refs[n_top:])):
        part = pl.ds(side * half, half)
        total = terms[0][...].astype(jnp.float32)
        for term in terms[1:]:
            total += term[...].astype(jnp.float32)
        tmp_ref[part] = (base_ref[part].astype(jnp.float32) + total).astype(tmp_ref.dtype)
        copy = pltpu.make_async_copy(tmp_ref.at[part], out_ref.at[part], sem_ref.at[side])
        copy.start()
        copies.append(copy)
    for copy in copies:
        copy.wait()


def add_all(base, top, bottom):
    return pl.pallas_call(
        functools.partial(add_kernel, len(top)),
        out_shape=jax.ShapeDtypeStruct(base.shape, jnp.bfloat16),
        in_specs=vmem_specs(1 + len(top) + len(bottom)),
        out_specs=pl.BlockSpec(memory_space=pl.ANY),
        scratch_shapes=[pltpu.VMEM(base.shape, jnp.bfloat16), pltpu.SemaphoreType.DMA((2,))],
        compiler_params=params(16),
        cost_estimate=TINY,
    )(base, *top, *bottom)


def scatter_terms(parts, n):
    acc = {s: [[parts[s][0]], [parts[s][1]]] for s in range(n)}
    for s in by_bits(n, reverse=True):
        for side, bit in ((0, low_bit(s)), (1, high_bit(s))):
            terms = [t.astype(jnp.float32) for t in acc[s][side]]
            out = functools.reduce(lambda a, b: a + b, terms).astype(jnp.bfloat16)
            acc[s ^ bit][side].append(swap(out, bit))
    return acc[0]


def body(text, patches, grids, image_request, slot_start, vis_gain, dec_gain, w_qkv, w_out):
    n_req = lax.axis_size("req")
    n_ten = lax.axis_size("tensor")
    me_req = lax.axis_index("req")
    me_ten = lax.axis_index("tensor")
    img_dev, side, _, width = patches.shape
    half = side // 2
    region = half * half
    length = text.shape[0]
    w3 = jnp.transpose(w_qkv, (1, 0, 2))
    req_at = me_req.astype(jnp.int32)[None]
    ten_at = me_ten.astype(jnp.int32)[None]
    gains = dec_gain.astype(jnp.float32).reshape(n_ten, 1, width)
    order = by_bits(n_ten)
    near_at, far = order[:-1], order[-1]

    text_halves = split_rows(text)
    blocks = gather_halves(*text_halves, n_ten)

    outgoing = pool_images(req_at, image_request, jnp.transpose(patches, (1, 2, 0, 3)), n_req)
    received = [outgoing[0]] + [swap(outgoing[s], s, "req") for s in range(1, n_req)]

    n_rows = n_req * region
    n_img = round_up(n_rows + 1, 16)
    place, text_row, key_ok = placement(
        req_at, image_request, slot_start, grids, n_req, half, length, n_img
    )
    text_halves, outgoing = lax.optimization_barrier((text_halves, outgoing))
    acc, ss, w3 = own_part(ten_at, text_halves, gains, w3, n_ten)
    received, place, acc = lax.optimization_barrier((received, place, acc))

    img_own = pack_images(received, vis_gain.astype(jnp.float32).reshape(1, width), region, n_img)
    img_blocks = [img_own] + [swap(img_own, s) for s in range(1, n_ten)]

    near = [blocks[s] for s in near_at]
    acc, ss, w_out = near_part(near_at, ten_at, near, gains, w3, acc, ss, w_out)
    img_blocks, near = lax.optimization_barrier((img_blocks, near))
    img_qkv, merged = image_part(ten_at, img_blocks, gains, w3, n_rows)
    context, far_top, far_bottom = final_part(
        far, ten_at, blocks[far], gains, w3, acc, ss, img_qkv, place, text_row, key_ok, w_out
    )
    img_here = jnp.dot(place, merged, preferred_element_type=jnp.float32)
    x_in = (text.astype(jnp.float32) * text_row[:, :1] + img_here).astype(jnp.bfloat16)

    parts = {far: (far_top, far_bottom)}
    for s in reversed([0] + near_at):
        parts[s] = out_part(s, ten_at, context, w_out, width, jnp.float32 if s == 0 else jnp.bfloat16)
    top, bottom = scatter_terms(parts, n_ten)
    return add_all(x_in, top, bottom)


def solution(mesh):
    in_specs = (
        P("req", "tensor"),
        P("req", None, None, "tensor"),
        P(),
        P(),
        P(),
        P("tensor"),
        P(),
        P(None, None, "tensor"),
        P("tensor", None),
    )
    out_specs = P("req", "tensor")
    return jax.shard_map(body, mesh=mesh, in_specs=in_specs, out_specs=out_specs, check_vma=False)
```

time: 80.4 us -> 96.3 us (1.20)
  waiting for transfers between devices: 23.2 us -> 43.2 us
  local copies, waits for them, and re-layouts: 13.8 us -> 3.93 us
  starting transfers between devices: 22 us -> 26.4 us
  Pallas kernels: 17.6 us -> 20.2 us
    ppermute x15 -> x22, waiting for transfers between devices: 23.2 us -> 43.2 us  [swap(): return lax.ppermute(x, axis, [(i, i ^ s) for i in range(n)])]
    ppermute x15 -> x22, starting transfers between devices: 16.7 us -> 26.4 us  [swap(): return lax.ppermute(x, axis, [(i, i ^ s) for i in range(n)])]
    unnamed x12 -> x10, local copies, waits for them, and re-layouts: 9.42 us -> 3.03 us
    all_to_all x1 -> x0, starting transfers between devices: 5.31 us -> none  [body(): lax.all_to_all(outgoing, 'req', split_axis=0, concat_axis=0, tiled=True)]
    pallas_call x8 -> x9, Pallas kernels: 12.9 us -> 16.4 us  [the longest x1 4.76 us: own_part(): pl.pallas_call(functools.partial(own_kernel, n_ten), out_shape=(jax.Shape...]
    reshape x3 -> x0, local copies, waits for them, and re-layouts: 2.23 us -> none  [the longest x1 0.76 us: body(): grids.reshape(n_req, img_dev, 2)]
    slice x1, local copies, waits for them, and re-layouts: 1.17 us -> 0.14 us  [body(): text_row[:, :1]]
  transfers between devices with their start and end apart: 16 -> 22, of which waited for: 5 -> 6; matrix products, arithmetic and copies ran while one was open for 8% -> 3% of each run, Pallas kernels for 15% -> 15%
where the time goes in v3:
time: 96.3 us; the launch traced here: 96 us
  waiting for transfers between devices  43.2 us (45%)
  starting transfers between devices  26.4 us (27%)
  Pallas kernels  20.2 us (21%)
  local copies, waits for them, and re-layouts  3.93 us (4%)
  other arithmetic  1.65 us (2%)
    ppermute x22, waiting for transfers between devices, swap(): return lax.ppermute(x, axis, [(i, i ^ s) for i in range(n)])  43.2 us
    ppermute x22, starting transfers between devices, swap(): return lax.ppermute(x, axis, [(i, i ^ s) for i in range(n)])  26.4 us
    pallas_call x1, Pallas kernels, own_part(): pl.pallas_call(functools.partial(own_kernel, n_ten), out_shape=(jax.Shape...  4.76 us
    pallas_call x1, Pallas kernels, final_part(): pl.pallas_call(functools.partial(final_kernel, far), out_shape=(jax.Shape...  3.38 us
    unnamed x10, local copies, waits for them, and re-layouts  3.03 us
    pallas_call x1, Pallas kernels, near_part(): pl.pallas_call(functools.partial(near_kernel, near), out_shape=(jax.Shape...  2.9 us
    pallas_call x1, Pallas kernels, image_part(): pl.pallas_call(functools.partial(image_kernel, n_blk, n_rows), out_shape=...  2.6 us
  transfers between devices with their start and end apart: 22, of which 6 were waited for; matrix products, arithmetic and copies ran while one was open for 3% of the time, Pallas kernels for 15%

profile of v3, /device:TPU:0, one launch (start us, length us, event | category | flops | bytes accessed | tf_op | source)
XLA Modules:
  0.0 96.0 jit_solution(14433572572099492303)
XLA Ops:
  0.0 1.1 %shard_map.93 = (bf16[192,1024]{1,0:T(8,128)(2,1)S(1)}, bf16[192,1024]{1,0:T(8,128)(2,1)S(1)}) custom-call(bf16[384,1024]{1,0:T(8,128)(2,1)} %x_ref.1), custom_call_target="tpu_custom_call" | custom-call | tf_op jit(solution)/shard_map/pallas_call | solution.py:76
  1.1 3.0 %collective-permute-start.12 = (bf16[192,1024]{1,0:T(8,128)(2,1)S(1)}, bf16[192,1024]{1,0:T(8,128)(2,1)S(1)}, u32[]{:S(2)}, u32[]{:S(2)}) collective-permute-start(bf16[192,1024]{1,0:T(8,128)(2,1)S(1)} %get-tuple-element.63.top_ref), channel_id=1, source_target_pairs={{0,2},{1,3},{2,0},{3,1},{4,6},{5,7},{6,4},{7,5},{8,10},{9,11},{10,... | collective-permute-start | bytes 1179656 | tf_op jit(solution)/shard_map/ppermute | solution.py:23
  4.2 1.5 %collective-permute-start.11 = (bf16[192,1024]{1,0:T(8,128)(2,1)S(1)}, bf16[192,1024]{1,0:T(8,128)(2,1)S(1)}, u32[]{:S(2)}, u32[]{:S(2)}) collective-permute-start(bf16[192,1024]{1,0:T(8,128)(2,1)S(1)} %get-tuple-element.64.bottom_ref), channel_id=1, source_target_pairs={{0,1},{1,0},{2,3},{3,2},{4,5},{5,4},{6,7},{7,6},{8,9},{9,8},{10,11... | collective-permute-start | bytes 1179656 | tf_op jit(solution)/shard_map/ppermute | solution.py:23
  5.7 1.1 %copy-done = bf16[8,6,6,1024]{3,0,2,1:T(8,128)(2,1)S(1)} copy-done((bf16[8,6,6,1024]{3,0,2,1:T(8,128)(2,1)S(1)}, bf16[8,6,6,1024]{3,0,2,1:T(8,128)(2,1)}, u32[]{:S(2)}) %copy-start) | copy-done | bytes 589848
  6.7 0.7 copy-done.1
  7.4 0.8 shard_map.92
  8.2 0.1 collective-permute-start
  8.3 1.6 %collective-permute-start.1 = (bf16[16,1024]{1,0:T(8,128)(2,1)S(1)}, bf16[16,1024]{1,0:T(8,128)(2,1)S(1)}, u32[]{:S(2)}, u32[]{:S(2)}) collective-permute-start(bf16[16,1024]{1,0:T(8,128)(2,1)S(1)} %get-tuple-element.54), channel_id=1, source_target_pairs={{0,8},{4,12},{8,0},{12,4},{16,24},{20,28},{24,16},{28,20},{1,9},{5... | collective-permute-start | bytes 98312 | tf_op jit(solution)/shard_map/ppermute | solution.py:23
  10.0 0.2 collective-permute-start.2
  10.2 0.0 collective-permute-done.refs_1_
  10.2 2.6 %collective-permute-start.3 = (bf16[16,1024]{1,0:T(8,128)(2,1)S(1)}, bf16[16,1024]{1,0:T(8,128)(2,1)S(1)}, u32[]{:S(2)}, u32[]{:S(2)}) collective-permute-start(bf16[16,1024]{1,0:T(8,128)(2,1)S(1)} %get-tuple-element.56), channel_id=1, source_target_pairs={{0,16},{4,20},{8,24},{12,28},{16,0},{20,4},{24,8},{28,12},{1,17},{... | collective-permute-start | bytes 98312 | tf_op jit(solution)/shard_map/ppermute | solution.py:23
  12.8 0.0 collective-permute-done.1.refs_2_
  12.8 1.3 %collective-permute-start.4 = (bf16[16,1024]{1,0:T(8,128)(2,1)S(1)}, bf16[16,1024]{1,0:T(8,128)(2,1)S(1)}, u32[]{:S(2)}, u32[]{:S(2)}) collective-permute-start(bf16[16,1024]{1,0:T(8,128)(2,1)S(1)} %get-tuple-element.57), channel_id=1, source_target_pairs={{0,20},{4,16},{8,28},{12,24},{16,4},{20,0},{24,12},{28,8},{1,21},{... | collective-permute-start | bytes 98312 | tf_op jit(solution)/shard_map/ppermute | solution.py:23
  14.1 0.0 collective-permute-done.2.refs_3_
  14.1 2.3 %collective-permute-start.5 = (bf16[16,1024]{1,0:T(8,128)(2,1)S(1)}, bf16[16,1024]{1,0:T(8,128)(2,1)S(1)}, u32[]{:S(2)}, u32[]{:S(2)}) collective-permute-start(bf16[16,1024]{1,0:T(8,128)(2,1)S(1)} %get-tuple-element.58), channel_id=1, source_target_pairs={{0,24},{4,28},{8,16},{12,20},{16,8},{20,12},{24,0},{28,4},{1,25},{... | collective-permute-start | bytes 98312 | tf_op jit(solution)/shard_map/ppermute | solution.py:23
  16.4 0.0 collective-permute-done.3.refs_4_
  16.4 2.0 %collective-permute-start.6 = (bf16[16,1024]{1,0:T(8,128)(2,1)S(1)}, bf16[16,1024]{1,0:T(8,128)(2,1)S(1)}, u32[]{:S(2)}, u32[]{:S(2)}) collective-permute-start(bf16[16,1024]{1,0:T(8,128)(2,1)S(1)} %get-tuple-element.59), channel_id=1, source_target_pairs={{0,28},{4,24},{8,20},{12,16},{16,12},{20,8},{24,4},{28,0},{1,29},{... | collective-permute-start | bytes 98312 | tf_op jit(solution)/shard_map/ppermute | solution.py:23
  18.4 0.8 slice_bitcast_fusion
  19.1 0.7 reshape.14
  19.8 0.7 reshape.16
  20.5 0.7 copy-done.2
  21.2 0.7 copy-done.3
  21.8 1.6 %shard_map.91 = (bf16[384,80]{1,0:T(8,128)(2,1)S(1)}, f32[384,128]{1,0:T(8,128)S(1)}, f32[8,384]{1,0:T(8,128)S(1)}) custom-call(s32[1]{0:T(128)} %bitcast.me_ref, s32[64]{0:T(128)S(1)} %copy-done.2, s32[64]{0:T(128)S(1)} %copy-done.3, s32[64]{0:T(128)S(1)} %get-tuple-element.98.high_ref, s32[64]{0:T(128)S(1)} %get-tuple-element.97.wide_ref), custom_call_target="tpu_custom_call" | custom-call | tf_op jit(solution)/shard_map/pallas_call | solution.py:191
  23.4 4.8 %shard_map.94 = (f32[3,384,512]{2,1,0:T(8,128)S(1)}, f32[384,128]{1,0:T(8,128)S(1)}, bf16[3,4096,512]{2,1,0:T(8,128)(2,1)S(1)}) custom-call(s32[1]{0:T(128)} %bitcast.4.me_ref, bf16[192,1024]{1,0:T(8,128)(2,1)S(1)} %get-tuple-element.63.top_ref, bf16[192,1024]{1,0:T(8,128)(2,1)S(1)} %get-tuple-element.64.bottom_ref, f32[4,1,1024]{2,1,0:T(1,128)S(1)} %bitcast.13, ...), custom_call_target="tpu_custom_call" | custom-call | tf_op jit(solution)/shard_map/pallas_call | solution.py:245
  28.2 0.0 collective-permute-done.5.refs_6_
  28.2 0.0 collective-permute-done.6.refs_7_
  28.3 0.1 shard_map.95.refs_0_
  28.3 0.6 collective-permute-start.7
  28.9 1.5 %collective-permute-start.10 = (bf16[192,1024]{1,0:T(8,128)(2,1)S(1)}, bf16[192,1024]{1,0:T(8,128)(2,1)S(1)}, u32[]{:S(2)}, u32[]{:S(2)}) collective-permute-start(bf16[192,1024]{1,0:T(8,128)(2,1)S(1)} %get-tuple-element.63.top_ref), channel_id=1, source_target_pairs={{0,1},{1,0},{2,3},{3,2},{4,5},{5,4},{6,7},{7,6},{8,9},{9,8},{10,11... | collective-permute-start | bytes 1179656 | tf_op jit(solution)/shard_map/ppermute | solution.py:23
  30.4 0.5 collective-permute-start.13
  30.9 0.0 collective-permute-done.12.refs_2_
  30.9 0.5 collective-permute-start.14
  31.5 0.0 collective-permute-done.11.refs_1_
  31.5 1.5 %collective-permute-start.15 = (bf16[192,1024]{1,0:T(8,128)(2,1)S(1)}, bf16[192,1024]{1,0:T(8,128)(2,1)S(1)}, u32[]{:S(2)}, u32[]{:S(2)}) collective-permute-start(bf16[192,1024]{1,0:T(8,128)(2,1)S(1)} %collective-permute-done.11.refs_1_), channel_id=1, source_target_pairs={{0,2},{1,3},{2,0},{3,1},{4,6},{5,7},{6,4},{7,5},{8,10},{9,11},{10,... | collective-permute-start | bytes 1179656 | tf_op jit(solution)/shard_map/ppermute | solution.py:23
  33.0 2.4 %collective-permute-done.7.refs_1_ = bf16[80,1024]{1,0:T(8,128)(2,1)S(1)} collective-permute-done((bf16[80,1024]{1,0:T(8,128)(2,1)S(1)}, bf16[80,1024]{1,0:T(8,128)(2,1)S(1)}, u32[]{:S(2)}, u32[]{:S(2)}) %collective-permute-start.7) | collective-permute-done | bytes 163872 | tf_op jit(solution)/shard_map/ppermute | solution.py:23
  35.5 0.5 collective-permute-start.8
  36.0 17.5 %collective-permute-done.8.refs_2_ = bf16[80,1024]{1,0:T(8,128)(2,1)S(1)} collective-permute-done((bf16[80,1024]{1,0:T(8,128)(2,1)S(1)}, bf16[80,1024]{1,0:T(8,128)(2,1)S(1)}, u32[]{:S(2)}, u32[]{:S(2)}) %collective-permute-start.8) | collective-permute-done | bytes 163872 | tf_op jit(solution)/shard_map/ppermute | solution.py:23
  53.5 0.5 collective-permute-start.9
  54.0 5.8 %collective-permute-done.9.refs_3_ = bf16[80,1024]{1,0:T(8,128)(2,1)S(1)} collective-permute-done((bf16[80,1024]{1,0:T(8,128)(2,1)S(1)}, bf16[80,1024]{1,0:T(8,128)(2,1)S(1)}, u32[]{:S(2)}, u32[]{:S(2)}) %collective-permute-start.9) | collective-permute-done | bytes 163872 | tf_op jit(solution)/shard_map/ppermute | solution.py:23
  59.7 0.0 collective-permute-done.10.refs_0_
  59.7 0.0 collective-permute-done.13.refs_3_
  59.7 2.6 %shard_map.96 = (bf16[3,80,512]{2,1,0:T(8,128)(2,1)S(1)}, bf16[80,1024]{1,0:T(8,128)(2,1)S(1)}) custom-call(s32[1]{0:T(128)} %bitcast.4.me_ref, bf16[80,1024]{1,0:T(8,128)(2,1)S(1)} %shard_map.95.refs_0_, bf16[80,1024]{1,0:T(8,128)(2,1)S(1)} %collective-permute-done.7.refs_1_, bf16[80,1024]{1,0:T(8,128)(2,1)S(1)} %collective-permute-done.8.refs_2_, ...), custom_call_target="tpu_custom_call" | custom-call | tf_op jit(solution)/shard_map/pallas_call | solution.py:337
  62.3 2.9 %shard_map.97 = (f32[3,384,512]{2,1,0:T(8,128)S(1)}, f32[384,128]{1,0:T(8,128)S(1)}, bf16[512,4096]{1,0:T(8,128)(2,1)S(1)}) custom-call(s32[1]{0:T(128)} %bitcast.4.me_ref, bf16[192,1024]{1,0:T(8,128)(2,1)S(1)} %collective-permute-done.10.refs_0_, bf16[192,1024]{1,0:T(8,128)(2,1)S(1)} %collective-permute-done.11.refs_1_, ...), custom_call_target="tpu_custom_call" | custom-call | tf_op jit(solution)/shard_map/pallas_call | solution.py:288
  65.2 0.0 collective-permute-done.15.bottom_ref
  65.3 3.4 %shard_map.98 = (bf16[384,512]{1,0:T(8,128)(2,1)S(1)}, bf16[192,1024]{1,0:T(8,128)(2,1)S(1)}, bf16[192,1024]{1,0:T(8,128)(2,1)S(1)}) custom-call(s32[1]{0:T(128)} %bitcast.4.me_ref, bf16[192,1024]{1,0:T(8,128)(2,1)S(1)} %collective-permute-done.14.top_ref, bf16[192,1024]{1,0:T(8,128)(2,1)S(1)} %collective-permute-done.15.bottom_ref, ...), custom_call_target="tpu_custom_call" | custom-call | tf_op jit(solution)/shard_map/pallas_call | solution.py:406
  68.6 0.6 collective-permute-start.20
  69.2 0.6 collective-permute-start.16
  69.8 0.6 shard_map.101
  70.4 0.6 shard_map.100
  71.0 0.0 copy-start.4
  71.0 1.5 %collective-permute-start.18 = (bf16[192,1024]{1,0:T(8,128)(2,1)S(1)}, bf16[192,1024]{1,0:T(8,128)(2,1)S(1)}, u32[]{:S(2)}, u32[]{:S(2)}) collective-permute-start(bf16[192,1024]{1,0:T(8,128)(2,1)S(1)} %get-tuple-element.92), channel_id=1, source_target_pairs={{0,1},{1,0},{2,3},{3,2},{4,5},{5,4},{6,7},{7,6},{8,9},{9,8},{10,11... | collective-permute-start | bytes 1179656 | tf_op jit(solution)/shard_map/ppermute | solution.py:23
  72.5 1.5 %collective-permute-start.19 = (bf16[192,1024]{1,0:T(8,128)(2,1)S(1)}, bf16[192,1024]{1,0:T(8,128)(2,1)S(1)}, u32[]{:S(2)}, u32[]{:S(2)}) collective-permute-start(bf16[192,1024]{1,0:T(8,128)(2,1)S(1)} %get-tuple-element.94), channel_id=1, source_target_pairs={{0,2},{1,3},{2,0},{3,1},{4,6},{5,7},{6,4},{7,5},{8,10},{9,11},{10,... | collective-permute-start | bytes 1179656 | tf_op jit(solution)/shard_map/ppermute | solution.py:23
  74.1 6.7 %collective-permute-done.20 = bf16[192,1024]{1,0:T(8,128)(2,1)S(1)} collective-permute-done((bf16[192,1024]{1,0:T(8,128)(2,1)S(1)}, bf16[192,1024]{1,0:T(8,128)(2,1)S(1)}, u32[]{:S(2)}, u32[]{:S(2)}) %collective-permute-start.20) | collective-permute-done | bytes 393248 | tf_op jit(solution)/shard_map/ppermute | solution.py:23
  80.8 0.1 add_convert_fusion.1
  80.9 0.6 collective-permute-start.21
  81.5 0.1 add_convert_fusion.2
  81.7 1.3 %collective-permute-start.17 = (bf16[192,1024]{1,0:T(8,128)(2,1)S(1)}, bf16[192,1024]{1,0:T(8,128)(2,1)S(1)}, u32[]{:S(2)}, u32[]{:S(2)}) collective-permute-start(bf16[192,1024]{1,0:T(8,128)(2,1)S(1)} %add_convert_fusion.2), channel_id=1, source_target_pairs={{0,2},{1,3},{2,0},{3,1},{4,6},{5,7},{6,4},{7,5},{8,10},{9,11},{10,... | collective-permute-start | bytes 1179656 | tf_op jit(solution)/shard_map/ppermute | solution.py:23
  83.0 0.1 slice_reduce_fusion
  83.1 0.4 add_convert_fusion.base_ref
  83.5 0.6 shard_map.99
  84.1 5.6 %collective-permute-done.18.refs_2_ = bf16[192,1024]{1,0:T(8,128)(2,1)S(1)} collective-permute-done((bf16[192,1024]{1,0:T(8,128)(2,1)S(1)}, bf16[192,1024]{1,0:T(8,128)(2,1)S(1)}, u32[]{:S(2)}, u32[]{:S(2)}) %collective-permute-start.18) | collective-permute-done | bytes 393248 | tf_op jit(solution)/shard_map/ppermute | solution.py:23
  89.7 0.0 collective-permute-done.19.refs_4_
  89.7 5.2 %collective-permute-done.21.refs_5_ = bf16[192,1024]{1,0:T(8,128)(2,1)S(1)} collective-permute-done((bf16[192,1024]{1,0:T(8,128)(2,1)S(1)}, bf16[192,1024]{1,0:T(8,128)(2,1)S(1)}, u32[]{:S(2)}, u32[]{:S(2)}) %collective-permute-start.21) | collective-permute-done | bytes 393248 | tf_op jit(solution)/shard_map/ppermute | solution.py:23
  94.9 1.1 %shard_map.102 = bf16[384,1024]{1,0:T(8,128)(2,1)} custom-call(bf16[384,1024]{1,0:T(8,128)(2,1)S(1)} %add_convert_fusion.base_ref, f32[192,1024]{1,0:T(8,128)S(1)} %get-tuple-element.89.refs_0_, bf16[192,1024]{1,0:T(8,128)(2,1)S(1)} %collective-permute-done.17.refs_1_, bf16[192,1024]{1,0:T(8,128)(2,1)S(1)} %collective-permute-done.18.refs_2_, ...), custom_call_target="tpu_custom_call" | custom-call | tf_op jit(solution)/shard_map/pallas_call | solution.py:465
  (9 shorter events, 0.0 us)
Async XLA Ops:
  1.1 29.8 %collective-permute-start.12 = (bf16[192,1024]{1,0:T(8,128)(2,1)S(1)}, bf16[192,1024]{1,0:T(8,128)(2,1)S(1)}, u32[]{:S(2)}, u32[]{:S(2)}) collective-permute-start(bf16[192,1024]{1,0:T(8,128)(2,1)S(1)} %get-tuple-element.63.top_ref), channel_id=1, source_target_pairs={{0,2},{1,3},{2,0},{3,1},{4,6},{5,7},{6,4},{7,5},{8,10},{9,11},{10,... | collective-permute-start | bytes 1179656 | tf_op jit(solution)/shard_map/ppermute | solution.py:23
  4.2 27.3 %collective-permute-start.11 = (bf16[192,1024]{1,0:T(8,128)(2,1)S(1)}, bf16[192,1024]{1,0:T(8,128)(2,1)S(1)}, u32[]{:S(2)}, u32[]{:S(2)}) collective-permute-start(bf16[192,1024]{1,0:T(8,128)(2,1)S(1)} %get-tuple-element.64.bottom_ref), channel_id=1, source_target_pairs={{0,1},{1,0},{2,3},{3,2},{4,5},{5,4},{6,7},{7,6},{8,9},{9,8},{10,11... | collective-permute-start | bytes 1179656 | tf_op jit(solution)/shard_map/ppermute | solution.py:23
  5.7 1.1 %copy-start = (bf16[8,6,6,1024]{3,0,2,1:T(8,128)(2,1)S(1)}, bf16[8,6,6,1024]{3,0,2,1:T(8,128)(2,1)}, u32[]{:S(2)}) copy-start(bf16[8,6,6,1024]{3,0,2,1:T(8,128)(2,1)} %param.10) | copy-start | bytes 1769476
  6.7 0.7 copy-start.1
  8.2 1.9 %collective-permute-start = (bf16[16,1024]{1,0:T(8,128)(2,1)S(1)}, bf16[16,1024]{1,0:T(8,128)(2,1)S(1)}, u32[]{:S(2)}, u32[]{:S(2)}) collective-permute-start(bf16[16,1024]{1,0:T(8,128)(2,1)S(1)} %get-tuple-element.53), channel_id=1, source_target_pairs={{0,4},{4,0},{8,12},{12,8},{16,20},{20,16},{24,28},{28,24},{1,5},{5... | collective-permute-start | bytes 98312 | tf_op jit(solution)/shard_map/ppermute | solution.py:23
  8.3 4.5 %collective-permute-start.1 = (bf16[16,1024]{1,0:T(8,128)(2,1)S(1)}, bf16[16,1024]{1,0:T(8,128)(2,1)S(1)}, u32[]{:S(2)}, u32[]{:S(2)}) collective-permute-start(bf16[16,1024]{1,0:T(8,128)(2,1)S(1)} %get-tuple-element.54), channel_id=1, source_target_pairs={{0,8},{4,12},{8,0},{12,4},{16,24},{20,28},{24,16},{28,20},{1,9},{5... | collective-permute-start | bytes 98312 | tf_op jit(solution)/shard_map/ppermute | solution.py:23
  10.0 4.1 %collective-permute-start.2 = (bf16[16,1024]{1,0:T(8,128)(2,1)S(1)}, bf16[16,1024]{1,0:T(8,128)(2,1)S(1)}, u32[]{:S(2)}, u32[]{:S(2)}) collective-permute-start(bf16[16,1024]{1,0:T(8,128)(2,1)S(1)} %get-tuple-element.55), channel_id=1, source_target_pairs={{0,12},{4,8},{8,4},{12,0},{16,28},{20,24},{24,20},{28,16},{1,13},{... | collective-permute-start | bytes 98312 | tf_op jit(solution)/shard_map/ppermute | solution.py:23
  10.2 6.2 %collective-permute-start.3 = (bf16[16,1024]{1,0:T(8,128)(2,1)S(1)}, bf16[16,1024]{1,0:T(8,128)(2,1)S(1)}, u32[]{:S(2)}, u32[]{:S(2)}) collective-permute-start(bf16[16,1024]{1,0:T(8,128)(2,1)S(1)} %get-tuple-element.56), channel_id=1, source_target_pairs={{0,16},{4,20},{8,24},{12,28},{16,0},{20,4},{24,8},{28,12},{1,17},{... | collective-permute-start | bytes 98312 | tf_op jit(solution)/shard_map/ppermute | solution.py:23
  12.8 15.4 %collective-permute-start.4 = (bf16[16,1024]{1,0:T(8,128)(2,1)S(1)}, bf16[16,1024]{1,0:T(8,128)(2,1)S(1)}, u32[]{:S(2)}, u32[]{:S(2)}) collective-permute-start(bf16[16,1024]{1,0:T(8,128)(2,1)S(1)} %get-tuple-element.57), channel_id=1, source_target_pairs={{0,20},{4,16},{8,28},{12,24},{16,4},{20,0},{24,12},{28,8},{1,21},{... | collective-permute-start | bytes 98312 | tf_op jit(solution)/shard_map/ppermute | solution.py:23
  14.1 14.2 %collective-permute-start.5 = (bf16[16,1024]{1,0:T(8,128)(2,1)S(1)}, bf16[16,1024]{1,0:T(8,128)(2,1)S(1)}, u32[]{:S(2)}, u32[]{:S(2)}) collective-permute-start(bf16[16,1024]{1,0:T(8,128)(2,1)S(1)} %get-tuple-element.58), channel_id=1, source_target_pairs={{0,24},{4,28},{8,16},{12,20},{16,8},{20,12},{24,0},{28,4},{1,25},{... | collective-permute-start | bytes 98312 | tf_op jit(solution)/shard_map/ppermute | solution.py:23
  16.4 11.9 %collective-permute-start.6 = (bf16[16,1024]{1,0:T(8,128)(2,1)S(1)}, bf16[16,1024]{1,0:T(8,128)(2,1)S(1)}, u32[]{:S(2)}, u32[]{:S(2)}) collective-permute-start(bf16[16,1024]{1,0:T(8,128)(2,1)S(1)} %get-tuple-element.59), channel_id=1, source_target_pairs={{0,28},{4,24},{8,20},{12,16},{16,12},{20,8},{24,4},{28,0},{1,29},{... | collective-permute-start | bytes 98312 | tf_op jit(solution)/shard_map/ppermute | solution.py:23
  20.5 0.7 copy-start.2
  21.2 0.7 copy-start.3
  28.3 7.1 %collective-permute-start.7 = (bf16[80,1024]{1,0:T(8,128)(2,1)S(1)}, bf16[80,1024]{1,0:T(8,128)(2,1)S(1)}, u32[]{:S(2)}, u32[]{:S(2)}) collective-permute-start(bf16[80,1024]{1,0:T(8,128)(2,1)S(1)} %shard_map.95.refs_0_), channel_id=1, source_target_pairs={{0,1},{1,0},{2,3},{3,2},{4,5},{5,4},{6,7},{7,6},{8,9},{9,8},{10,11... | collective-permute-start | bytes 491528 | tf_op jit(solution)/shard_map/ppermute | solution.py:23
  28.9 30.8 %collective-permute-start.10 = (bf16[192,1024]{1,0:T(8,128)(2,1)S(1)}, bf16[192,1024]{1,0:T(8,128)(2,1)S(1)}, u32[]{:S(2)}, u32[]{:S(2)}) collective-permute-start(bf16[192,1024]{1,0:T(8,128)(2,1)S(1)} %get-tuple-element.63.top_ref), channel_id=1, source_target_pairs={{0,1},{1,0},{2,3},{3,2},{4,5},{5,4},{6,7},{7,6},{8,9},{9,8},{10,11... | collective-permute-start | bytes 1179656 | tf_op jit(solution)/shard_map/ppermute | solution.py:23
  30.4 29.3 %collective-permute-start.13 = (bf16[192,1024]{1,0:T(8,128)(2,1)S(1)}, bf16[192,1024]{1,0:T(8,128)(2,1)S(1)}, u32[]{:S(2)}, u32[]{:S(2)}) collective-permute-start(bf16[192,1024]{1,0:T(8,128)(2,1)S(1)} %get-tuple-element.64.bottom_ref), channel_id=1, source_target_pairs={{0,2},{1,3},{2,0},{3,1},{4,6},{5,7},{6,4},{7,5},{8,10},{9,11},{10,... | collective-permute-start | bytes 1179656 | tf_op jit(solution)/shard_map/ppermute | solution.py:23
  30.9 34.3 %collective-permute-start.14 = (bf16[192,1024]{1,0:T(8,128)(2,1)S(1)}, bf16[192,1024]{1,0:T(8,128)(2,1)S(1)}, u32[]{:S(2)}, u32[]{:S(2)}) collective-permute-start(bf16[192,1024]{1,0:T(8,128)(2,1)S(1)} %collective-permute-done.12.refs_2_), channel_id=1, source_target_pairs={{0,1},{1,0},{2,3},{3,2},{4,5},{5,4},{6,7},{7,6},{8,9},{9,8},{10,11... | collective-permute-start | bytes 1179656 | tf_op jit(solution)/shard_map/ppermute | solution.py:23
  31.5 33.8 %collective-permute-start.15 = (bf16[192,1024]{1,0:T(8,128)(2,1)S(1)}, bf16[192,1024]{1,0:T(8,128)(2,1)S(1)}, u32[]{:S(2)}, u32[]{:S(2)}) collective-permute-start(bf16[192,1024]{1,0:T(8,128)(2,1)S(1)} %collective-permute-done.11.refs_1_), channel_id=1, source_target_pairs={{0,2},{1,3},{2,0},{3,1},{4,6},{5,7},{6,4},{7,5},{8,10},{9,11},{10,... | collective-permute-start | bytes 1179656 | tf_op jit(solution)/shard_map/ppermute | solution.py:23
  35.5 18.0 %collective-permute-start.8 = (bf16[80,1024]{1,0:T(8,128)(2,1)S(1)}, bf16[80,1024]{1,0:T(8,128)(2,1)S(1)}, u32[]{:S(2)}, u32[]{:S(2)}) collective-permute-start(bf16[80,1024]{1,0:T(8,128)(2,1)S(1)} %shard_map.95.refs_0_), channel_id=1, source_target_pairs={{0,2},{1,3},{2,0},{3,1},{4,6},{5,7},{6,4},{7,5},{8,10},{9,11},{10,... | collective-permute-start | bytes 491528 | tf_op jit(solution)/shard_map/ppermute | solution.py:23
  53.5 6.2 %collective-permute-start.9 = (bf16[80,1024]{1,0:T(8,128)(2,1)S(1)}, bf16[80,1024]{1,0:T(8,128)(2,1)S(1)}, u32[]{:S(2)}, u32[]{:S(2)}) collective-permute-start(bf16[80,1024]{1,0:T(8,128)(2,1)S(1)} %shard_map.95.refs_0_), channel_id=1, source_target_pairs={{0,3},{1,2},{2,1},{3,0},{4,7},{5,6},{6,5},{7,4},{8,11},{9,10},{10,... | collective-permute-start | bytes 491528 | tf_op jit(solution)/shard_map/ppermute | solution.py:23
  68.6 12.1 %collective-permute-start.20 = (bf16[192,1024]{1,0:T(8,128)(2,1)S(1)}, bf16[192,1024]{1,0:T(8,128)(2,1)S(1)}, u32[]{:S(2)}, u32[]{:S(2)}) collective-permute-start(bf16[192,1024]{1,0:T(8,128)(2,1)S(1)} %get-tuple-element.96), channel_id=1, source_target_pairs={{0,2},{1,3},{2,0},{3,1},{4,6},{5,7},{6,4},{7,5},{8,10},{9,11},{10,... | collective-permute-start | bytes 1179656 | tf_op jit(solution)/shard_map/ppermute | solution.py:23
  69.2 12.3 %collective-permute-start.16 = (bf16[192,1024]{1,0:T(8,128)(2,1)S(1)}, bf16[192,1024]{1,0:T(8,128)(2,1)S(1)}, u32[]{:S(2)}, u32[]{:S(2)}) collective-permute-start(bf16[192,1024]{1,0:T(8,128)(2,1)S(1)} %get-tuple-element.91), channel_id=1, source_target_pairs={{0,1},{1,0},{2,3},{3,2},{4,5},{5,4},{6,7},{7,6},{8,9},{9,8},{10,11... | collective-permute-start | bytes 1179656 | tf_op jit(solution)/shard_map/ppermute | solution.py:23
  71.0 12.2 %copy-start.4 = (bf16[384,1024]{1,0:T(8,128)(2,1)S(1)}, bf16[384,1024]{1,0:T(8,128)(2,1)}, u32[]{:S(2)}) copy-start(bf16[384,1024]{1,0:T(8,128)(2,1)} %x_ref.1) | copy-start | bytes 2359300
  71.0 18.7 %collective-permute-start.18 = (bf16[192,1024]{1,0:T(8,128)(2,1)S(1)}, bf16[192,1024]{1,0:T(8,128)(2,1)S(1)}, u32[]{:S(2)}, u32[]{:S(2)}) collective-permute-start(bf16[192,1024]{1,0:T(8,128)(2,1)S(1)} %get-tuple-element.92), channel_id=1, source_target_pairs={{0,1},{1,0},{2,3},{3,2},{4,5},{5,4},{6,7},{7,6},{8,9},{9,8},{10,11... | collective-permute-start | bytes 1179656 | tf_op jit(solution)/shard_map/ppermute | solution.py:23
  72.5 17.2 %collective-permute-start.19 = (bf16[192,1024]{1,0:T(8,128)(2,1)S(1)}, bf16[192,1024]{1,0:T(8,128)(2,1)S(1)}, u32[]{:S(2)}, u32[]{:S(2)}) collective-permute-start(bf16[192,1024]{1,0:T(8,128)(2,1)S(1)} %get-tuple-element.94), channel_id=1, source_target_pairs={{0,2},{1,3},{2,0},{3,1},{4,6},{5,7},{6,4},{7,5},{8,10},{9,11},{10,... | collective-permute-start | bytes 1179656 | tf_op jit(solution)/shard_map/ppermute | solution.py:23
  80.9 14.0 %collective-permute-start.21 = (bf16[192,1024]{1,0:T(8,128)(2,1)S(1)}, bf16[192,1024]{1,0:T(8,128)(2,1)S(1)}, u32[]{:S(2)}, u32[]{:S(2)}) collective-permute-start(bf16[192,1024]{1,0:T(8,128)(2,1)S(1)} %add_convert_fusion.1), channel_id=1, source_target_pairs={{0,1},{1,0},{2,3},{3,2},{4,5},{5,4},{6,7},{7,6},{8,9},{9,8},{10,11... | collective-permute-start | bytes 1179656 | tf_op jit(solution)/shard_map/ppermute | solution.py:23
  81.7 13.2 %collective-permute-start.17 = (bf16[192,1024]{1,0:T(8,128)(2,1)S(1)}, bf16[192,1024]{1,0:T(8,128)(2,1)S(1)}, u32[]{:S(2)}, u32[]{:S(2)}) collective-permute-start(bf16[192,1024]{1,0:T(8,128)(2,1)S(1)} %add_convert_fusion.2), channel_id=1, source_target_pairs={{0,2},{1,3},{2,0},{3,1},{4,6},{5,7},{6,4},{7,5},{8,10},{9,11},{10,... | collective-permute-start | bytes 1179656 | tf_op jit(solution)/shard_map/ppermute | solution.py:23
